TPU v7x, 32 devices: a whole 2x2x4 slice. The times are simulated.
32 devices in a mesh: dp: 4 (over y, core), seq: 8 (over z, x).
Axes of the slice: x: 2, y: 2, z: 4, core: 2. Of those that a mesh axis runs over, the one named last changes fastest.
Arguments:
- hidden: bfloat16 [8, 512, 2048], P('dp', 'seq'), may hold values from -6 to 6
- segments: int32 [8, 512], P('dp', 'seq'), may hold values from 0 to 3, never falling along the last dimension, each value on 1 to 256 neighbouring positions
- in_weight: bfloat16 [2048, 8512], P(('dp', 'seq')), may hold values from -0.125 to 0.125
- conv_weight: float32 [4352, 4], replicated, may hold values from -3 to 3
- conv_bias: float32 [4352], replicated, may hold values from -2 to 2
- dt_bias: float32 [64], replicated, may hold values from -6 to -2
- a_log: float32 [64], replicated, may hold values from 0 to 2.8
- d_skip: float32 [64], replicated, may hold values from 0.5 to 1.5
- norm_gain: float32 [2048], replicated, may hold values from 0.5 to 1.5
- gate_gain: float32 [4096], replicated, may hold values from 0.5 to 1.5
- out_weight: bfloat16 [4096, 2048], P(('dp', 'seq')), may hold values from -0.09375 to 0.09375
- cotangent: bfloat16 [8, 512, 2048], P('dp', 'seq'), may hold values from -6 to 6
Outputs:
- result: bfloat16 [8, 512, 2048], P('dp', 'seq')
- d_hidden: bfloat16 [8, 512, 2048], P('dp', 'seq')
- grad_in_weight: float32 [2048, 8512], P(('dp', 'seq'))
- grad_conv_weight: float32 [4352, 4], replicated
- grad_conv_bias: float32 [4352], replicated
- grad_dt_bias: float32 [64], replicated
- grad_a_log: float32 [64], replicated
- grad_d_skip: float32 [64], replicated
- grad_norm_gain: float32 [2048], replicated
- grad_gate_gain: float32 [4096], replicated
- grad_out_weight: float32 [4096, 2048], P(('dp', 'seq'))
Inputs may be any that keep to these rules, and one draw needn't show every extreme that they name: `segments`: within a sequence the document numbers start at 0, never fall and rise by at most one from a token to the next; every document has 1 to 256 tokens and one has exactly 256.
All inputs are finite; a program needn't handle non-finite values.
Results may differ from a plain program's by a relative error of at most 0.012.
The roundings to bfloat16 on the way count: a program that leaves them out, or rounds other values in their place, can miss the bound.
Values may be sent and summed in bfloat16 or wider, within the bound.
A program may use at most 320 MiB of HBM per device.

v0:
```python
import jax
import jax.numpy as jnp
from jax import lax
from jax.sharding import PartitionSpec as P

HEADS = 64
HDIM = 64
NST = 128
GROUP = 256
DI = 4096


def pre_norm(hidden_f, gain_vec):
    return (
        hidden_f
        * lax.rsqrt(jnp.mean(hidden_f * hidden_f, axis=-1, keepdims=True) + 1e-05)
        * gain_vec
    )


def gate_norm(y_values, gate_values, gain_vec):
    product = y_values * jax.nn.silu(gate_values)
    return (
        product * lax.rsqrt(jnp.mean(product * product, axis=-1, keepdims=True) + 1e-05) * gain_vec
    )


def conv_reset(signal, kernel, offset, seg_ids):
    tap_count = kernel.shape[1]
    summed = offset[None, :] + kernel[None, :, tap_count - 1] * signal
    for lag_steps in range(1, tap_count):
        shifted = jnp.pad(signal, ((lag_steps, 0), (0, 0)))[:-lag_steps]
        earlier = jnp.pad(seg_ids, (lag_steps, 0), constant_values=-1)[:-lag_steps]
        matches = (earlier == seg_ids).astype(jnp.float32)
        summed = summed + kernel[None, :, tap_count - 1 - lag_steps] * shifted * matches[:, None]
    return summed


def state_scan(values, deltas, rates, b_mat, c_mat, seg_ids):
    length, head_count, head_width = values.shape
    block_count = length // GROUP
    log_decay = deltas * rates[None, :]
    pieces = (
        values.reshape(block_count, GROUP, head_count, head_width),
        deltas.reshape(block_count, GROUP, head_count),
        log_decay.reshape(block_count, GROUP, head_count),
        b_mat.reshape(block_count, GROUP, b_mat.shape[-1]),
        c_mat.reshape(block_count, GROUP, c_mat.shape[-1]),
        seg_ids.reshape(block_count, GROUP),
    )
    position = lax.broadcasted_iota(jnp.int32, (GROUP, GROUP), 0)
    source = lax.broadcasted_iota(jnp.int32, (GROUP, GROUP), 1)

    def advance(carry, piece):
        memory, ending = carry
        block_vals, block_dt, block_log, b_block, c_block, seg_block = piece
        cumulative = jnp.cumsum(block_log, axis=0).T
        causal = (source <= position) & (seg_block[:, None] == seg_block[None, :])
        spread = cumulative[:, :, None] - cumulative[:, None, :]
        decays = jnp.where(causal[None], jnp.exp(jnp.where(causal[None], spread, 0.0)), 0.0)
        inner_prod = jnp.dot(c_block, b_block.T, precision=lax.Precision.HIGHEST)
        scores = inner_prod[None] * decays * block_dt.T[:, None, :]
        output = jnp.einsum("hij,jhp->ihp", scores, block_vals, precision=lax.Precision.HIGHEST)
        follows = (seg_block == ending).astype(jnp.float32)
        carried = jnp.einsum("in,hpn->ihp", c_block, memory, precision=lax.Precision.HIGHEST)
        output = output + (jnp.exp(cumulative).T * follows[:, None])[:, :, None] * carried
        last_seg = seg_block[-1]
        weights = (
            jnp.exp(cumulative[:, -1:] - cumulative)
            * (seg_block == last_seg).astype(jnp.float32)[None, :]
            * block_dt.T
        )
        keep_on = jnp.exp(cumulative[:, -1]) * (last_seg == ending).astype(jnp.float32)
        memory = memory * keep_on[:, None, None] + jnp.einsum(
            "hj,jhp,jn->hpn", weights, block_vals, b_block, precision=lax.Precision.HIGHEST
        )
        return ((memory, last_seg), output)

    initial = (
        jnp.zeros((head_count, head_width, b_mat.shape[-1]), jnp.float32),
        jnp.array(-1, jnp.int32),
    )
    unused, outputs = lax.scan(jax.checkpoint(advance), initial, pieces)
    return outputs.reshape(length, head_count, head_width)


def mixer(
    x_values,
    step_raw,
    bc_values,
    seg_ids,
    kernel_x,
    offset_x,
    kernel_bc,
    offset_bc,
    dt_shift,
    decay_log,
    skip_gain,
):
    x_conv = jax.nn.silu(conv_reset(x_values, kernel_x, offset_x, seg_ids))
    bc_conv = jax.nn.silu(conv_reset(bc_values, kernel_bc, offset_bc, seg_ids))
    step_sizes = jax.nn.softplus(step_raw + dt_shift[None, :])
    rates = -jnp.exp(decay_log)
    length = x_values.shape[0]
    head_count = step_raw.shape[1]
    shaped = x_conv.reshape(length, head_count, HDIM)
    mixed = (
        state_scan(shaped, step_sizes, rates, bc_conv[:, :NST], bc_conv[:, NST:], seg_ids)
        + skip_gain[None, :, None] * shaped
    )
    return mixed.reshape(length, head_count * HDIM)


def shards(
    hidden,
    segments,
    in_weight,
    conv_weight,
    conv_bias,
    dt_bias,
    a_log,
    d_skip,
    norm_gain,
    gate_gain,
    out_weight,
    cotangent,
):
    full_in, full_out = (
        lax.all_gather(in_weight, ("dp", "seq"), axis=0, tiled=True),
        lax.all_gather(out_weight, ("dp", "seq"), axis=0, tiled=True),
    )
    hidden_f = hidden.astype(jnp.float32)
    normed_f, pull_pre = jax.vjp(pre_norm, hidden_f, norm_gain)
    normed = normed_f.astype(jnp.bfloat16)
    project = jnp.einsum("mtd,df->mtf", normed, full_in, preferred_element_type=jnp.float32)
    gate_part = project[:, :, :DI]
    x_part = project[:, :, DI : 2 * DI].astype(jnp.bfloat16)
    bc_part = project[:, :, 2 * DI : 2 * DI + 2 * NST].astype(jnp.bfloat16)
    step_part = project[:, :, 2 * DI + 2 * NST :].astype(jnp.bfloat16)
    x_heads, step_heads = (
        lax.all_to_all(x_part, "seq", split_axis=2, concat_axis=1, tiled=True),
        lax.all_to_all(step_part, "seq", split_axis=2, concat_axis=1, tiled=True),
    )
    bc_full = lax.all_gather(bc_part, "seq", axis=1, tiled=True)
    seg_full = lax.all_gather(segments, "seq", axis=1, tiled=True)
    seq_rank = lax.axis_index("seq")
    head_local = step_heads.shape[2]
    chan_local = x_heads.shape[2]
    kernel_x = lax.dynamic_slice_in_dim(conv_weight, seq_rank * chan_local, chan_local, 0)
    offset_x = lax.dynamic_slice_in_dim(conv_bias, seq_rank * chan_local, chan_local, 0)
    shift_local = lax.dynamic_slice_in_dim(dt_bias, seq_rank * head_local, head_local, 0)
    decay_local = lax.dynamic_slice_in_dim(a_log, seq_rank * head_local, head_local, 0)
    skip_local = lax.dynamic_slice_in_dim(d_skip, seq_rank * head_local, head_local, 0)
    local_params = (
        kernel_x,
        offset_x,
        conv_weight[DI:],
        conv_bias[DI:],
        shift_local,
        decay_local,
        skip_local,
    )

    def head_mixer(x_values, step_raw, bc_values, params_in):

        def single_seq(x_one, step_one, bc_one, seg_one):
            return mixer(x_one, step_one, bc_one, seg_one, *params_in)

        return jax.vmap(single_seq)(x_values, step_raw, bc_values, seg_full)

    mixed, pull_mix = jax.vjp(
        head_mixer,
        x_heads.astype(jnp.float32),
        step_heads.astype(jnp.float32),
        bc_full.astype(jnp.float32),
        local_params,
    )
    y_tokens = lax.all_to_all(
        mixed.astype(jnp.bfloat16), "seq", split_axis=1, concat_axis=2, tiled=True
    )
    gated_f, pull_gate = jax.vjp(gate_norm, y_tokens.astype(jnp.float32), gate_part, gate_gain)
    gated = gated_f.astype(jnp.bfloat16)
    branch_out = jnp.einsum("mtf,fd->mtd", gated, full_out, preferred_element_type=jnp.float32)
    result = (hidden_f + branch_out).astype(jnp.bfloat16)
    d_gated = jnp.einsum("mtd,fd->mtf", cotangent, full_out, preferred_element_type=jnp.float32)
    d_mixed, d_gate_part, d_gate_gain = pull_gate(d_gated)
    d_heads = lax.all_to_all(
        d_mixed.astype(jnp.bfloat16), "seq", split_axis=2, concat_axis=1, tiled=True
    )
    d_x_heads, d_step_heads, d_bc_full, d_params = pull_mix(d_heads.astype(jnp.float32))
    d_x_part, d_step_part = (
        lax.all_to_all(
            d_x_heads.astype(jnp.bfloat16), "seq", split_axis=1, concat_axis=2, tiled=True
        ),
        lax.all_to_all(
            d_step_heads.astype(jnp.bfloat16), "seq", split_axis=1, concat_axis=2, tiled=True
        ),
    )
    d_bc_part = lax.psum_scatter(
        d_bc_full.astype(jnp.bfloat16), "seq", scatter_dimension=1, tiled=True
    )
    d_project = jnp.concatenate(
        [d_gate_part.astype(jnp.bfloat16), d_x_part, d_bc_part, d_step_part], axis=2
    )
    d_normed = jnp.einsum("mtf,df->mtd", d_project, full_in, preferred_element_type=jnp.float32)
    d_hidden_f, d_norm_gain = pull_pre(d_normed)
    d_hidden = (cotangent.astype(jnp.float32) + d_hidden_f).astype(jnp.bfloat16)
    in_rows = in_weight.shape[0]
    out_rows = out_weight.shape[0]
    column_ranges = ((0, DI), (DI, d_project.shape[2]))
    in_pieces = [jnp.zeros((in_rows, upper - lower), jnp.float32) for lower, upper in column_ranges]
    grad_out = jnp.zeros(out_weight.shape, jnp.float32)
    for batch_index in range(hidden.shape[0]):
        for range_index in range(len(column_ranges)):
            lower, upper = column_ranges[range_index]

            def in_term(
                start,
                count,
                normed_one=normed[batch_index],
                d_one=d_project[batch_index, :, lower:upper],
            ):
                return lax.dot_general(
                    normed_one, d_one, (((0,), (0,)), ((), ())), preferred_element_type=jnp.float32
                )

            in_pieces[range_index] = in_pieces[range_index] + lax.psum_scatter(
                in_term(jnp.int32(0), in_rows * lax.axis_size(("dp", "seq"))),
                ("dp", "seq"),
                scatter_dimension=0,
                tiled=True,
            )

        def out_term(start, count, gated_one=gated[batch_index], cot_one=cotangent[batch_index]):
            return lax.dot_general(
                gated_one, cot_one, (((0,), (0,)), ((), ())), preferred_element_type=jnp.float32
            )

        grad_out = grad_out + lax.psum_scatter(
            out_term(jnp.int32(0), out_rows * lax.axis_size(("dp", "seq"))),
            ("dp", "seq"),
            scatter_dimension=0,
            tiled=True,
        )
    grad_in = jnp.concatenate(in_pieces, axis=1)
    d_kernel_x, d_offset_x, d_kernel_bc, d_offset_bc, d_shift, d_decay, d_skip_part = d_params
    tap_count = conv_weight.shape[1]
    grad_conv_w = jnp.concatenate(
        [
            lax.dynamic_update_slice_in_dim(
                jnp.zeros((DI, tap_count), jnp.float32), d_kernel_x, seq_rank * chan_local, 0
            ),
            d_kernel_bc,
        ],
        axis=0,
    )
    grad_conv_b = jnp.concatenate(
        [
            lax.dynamic_update_slice_in_dim(
                jnp.zeros((DI,), jnp.float32), d_offset_x, seq_rank * chan_local, 0
            ),
            d_offset_bc,
        ],
        axis=0,
    )
    grad_shift = lax.dynamic_update_slice_in_dim(
        jnp.zeros((HEADS,), jnp.float32), d_shift, seq_rank * head_local, 0
    )
    grad_decay = lax.dynamic_update_slice_in_dim(
        jnp.zeros((HEADS,), jnp.float32), d_decay, seq_rank * head_local, 0
    )
    grad_skip = lax.dynamic_update_slice_in_dim(
        jnp.zeros((HEADS,), jnp.float32), d_skip_part, seq_rank * head_local, 0
    )
    totals = lax.psum(
        (grad_conv_w, grad_conv_b, grad_shift, grad_decay, grad_skip, d_norm_gain, d_gate_gain),
        ("dp", "seq"),
    )
    return (
        result,
        d_hidden,
        grad_in,
        totals[0],
        totals[1],
        totals[2],
        totals[3],
        totals[4],
        totals[5],
        totals[6],
        grad_out,
    )


def solution(mesh):
    placed = (
        P("dp", "seq", None),
        P("dp", "seq"),
        P(("dp", "seq"), None),
        P(),
        P(),
        P(),
        P(),
        P(),
        P(),
        P(),
        P(("dp", "seq"), None),
        P("dp", "seq", None),
    )
    return jax.shard_map(
        shards,
        mesh=mesh,
        in_specs=placed,
        out_specs=(
            P("dp", "seq", None),
            P("dp", "seq", None),
            P(("dp", "seq"), None),
            P(),
            P(),
            P(),
            P(),
            P(),
            P(),
            P(),
            P(("dp", "seq"), None),
        ),
        check_vma=False,
    )
```

profile of v0, /device:TPU:0, one launch (start us, length us, event | category | flops | bytes accessed | tf_op | source)
XLA Modules:
  0.0 3031.9 jit_solution(16363265577248465144)
XLA Ops:
  11.6 204.4 %all-gather.4.cloned.1.call-done = bf16[2048,8512]{1,0:T(8,128)(2,1)} async-done(((bf16[64,8512]{1,0:T(8,128)(2,1)}), bf16[2048,8512]{1,0:T(8,128)(2,1)}) %all-gather.4.cloned.1.call-update) | async-done | bytes 34865168 | tf_op jit(solution)/shard_map/all_gather | solution.py:129
  216.0 18.3 fusion.173
  254.9 44.8 %all-gather = s32[8,64,2]{1,2,0:T(2,128)S(1)} all-gather(s32[1,64,2]{1,2,0:T(2,128)S(1)} %bitcast.536), channel_id=1, replica_groups=mesh['dp'=4,'seq'=8] {'seq'}, dimensions={0}, use_global_device_ids=true | all-gather | bytes 4608 | tf_op jit(solution)/shard_map/all_gather | solution.py:145
  301.2 36.4 %all_gather.14 = bf16[2,512,256]{2,1,0:T(8,128)(2,1)S(1)} all-gather(bf16[2,64,256]{2,1,0:T(8,128)(2,1)S(1)} %slice.256), channel_id=1, replica_groups=mesh['dp'=4,'seq'=8] {'seq'}, dimensions={1}, use_global_device_ids=true | all-gather | bytes 589824 | tf_op jit(solution)/shard_map/all_gather | solution.py:144
  364.3 30.5 %while.46 = (s32[]{:T(128)}, f32[2,8,64,128]{3,2,1,0:T(8,128)S(1)}, s32[2]{0:T(128)S(1)}, f32[2,2,256,8,64]{2,4,3,1,0:T(8,128)}, f32[2,2,8,64,128]{4,3,2,1,0:T(8...) while((s32[]{:T(128)}, f32[2,8,64,128]{3,2,1,0:T(8,128)S(1)}, ...), condition=%wide.region_4.5_spmd.clone, body=%wide.region_1.4_spmd.clone.sunk | while | flops 1819494400 | bytes 27416212 | solution.py:83
  407.4 21.1 all_to_all.72
  432.8 14.2 multiply_reduce_fusion.4
  463.8 13.3 fusion.149
  477.1 9.4 all-to-all-done.3
  507.5 126.6 %while.47 = (s32[]{:T(128)}, f32[2,8,64,128]{3,2,1,0:T(8,128)}, f32[2,2,256,8,64]{2,4,3,1,0:T(8,128)}, f32[2,2,256,8]{2,0,3,1:T(2,128)}, f32[2,2,256,8]{2,0,3,1:...) while((s32[]{:T(128)}, f32[2,8,64,128]{3,2,1,0:T(8,128)}, ...), condition=%wide.region_19.20_spmd.clone, body=%wide.region_7.19_spmd.clone.sunk | while | flops 4253296640 | bytes 48230752 | solution.py:83
  538.3 7.8 fusion.258
  640.7 24.9 convolution_add_fusion.5
  693.9 31.4 %all-to-all-done.4 = bf16[2,512,512]{2,0,1:T(2,128)(2,1)S(1)} async-done(((bf16[2,512,512]{2,0,1:T(2,128)(2,1)}), bf16[2,512,512]{2,0,1:T(2,128)(2,1)S(1)}, u32[]{:S(2)}, u32[]{:S(2)}) %all-to-all-start.4) | async-done | bytes 1048608 | tf_op jit(solution)/shard_map/all_to_all | solution.py:192
  726.6 14.6 fusion.147
  741.3 26.7 convolution_add_fusion.4
  769.4 13.2 fusion.148
  783.3 24.9 convolution_add_fusion.6
  809.3 9.1 fusion.109
  819.7 16.8 fusion.139
  836.6 53.5 %all-reduce.27 = (f32[4352]{0:T(1024)}, f32[64]{0:T(128)}, f32[64]{0:T(128)}, f32[64]{0:T(128)}, f32[2048]{0:T(1024)}, /*index=5*/f32[4096]{0:T(1024)}) all-reduce(f32[4352]{0:T(1024)S(1)} %pad_maximum_fusion.3, f32[64]{0:T(128)S(1)} %dynamic_update_slice.85, ...), channel_id=1, replica_groups=mesh['dp'=4,'seq'=8] {'dp','seq'}, use_global_device_ids=true, to_apply=%region_37.38 | all-reduce | flops 10688 | bytes 85504 | tf_op jit(solution)/shard_map/psum | solution.py:275
  891.2 521.3 %reduce-scatter.7.cloned.1.call-done = f32[64,4096]{1,0:T(8,128)} async-done(((f32[2048,4096]{1,0:T(8,128)}), f32[64,4096]{1,0:T(8,128)}) %reduce-scatter.7.cloned.1.call-update) | async-done | bytes 1048592 | tf_op jit(solution)/shard_map/reduce_scatter | solution.py:227
  1412.5 774.8 %reduce-scatter.9.cloned.1.call-done = f32[64,4416]{1,0:T(8,128)} async-done(((f32[2048,4416]{1,0:T(8,128)}), f32[64,4416]{1,0:T(8,128)}) %reduce-scatter.9.cloned.1.call-update) | async-done | bytes 1130512 | tf_op jit(solution)/shard_map/reduce_scatter | solution.py:227
  2190.4 121.7 %all-reduce.30.cloned.1.call-done = f32[4352,4]{0,1:T(4,128)} async-done(((f32[4352,4]{0,1:T(4,128)}), f32[4352,4]{0,1:T(4,128)}) %all-reduce.30.cloned.1.call-update) | async-done | bytes 69648 | tf_op jit(solution)/shard_map/psum | solution.py:275
  2312.1 711.2 %reduce-scatter.11.cloned.1.call-done = f32[128,2048]{1,0:T(8,128)} async-done(((f32[4096,2048]{1,0:T(8,128)}), f32[128,2048]{1,0:T(8,128)}) %reduce-scatter.11.cloned.1.call-update) | async-done | bytes 1048592 | tf_op jit(solution)/shard_map/reduce_scatter | solution.py:239
  (534 shorter events, 301.3 us)
Async XLA Ops:
  7.2 208.8 %all-gather.4.cloned.1.call-start = ((), (), s32[]{:S(2)}) async-start(), calls=%async_computation.10 | async-start | bytes 36225024 | tf_op jit(solution)/shard_map/all_gather | solution.py:129
  7.9 424.8 %all-gather.6.cloned.1.call-start = ((), (), s32[]{:S(2)}) async-start(), calls=%async_computation.11 | async-start | bytes 17301504 | tf_op jit(solution)/shard_map/all_gather | solution.py:130
  11.4 327.2 %copy-start.78 = (f32[256,1]{0,1:T(1,128)}, f32[256,1]{0,1:T(1,128)S(1)}, u32[]{:S(2)}) copy-start(f32[256,1]{0,1:T(1,128)S(1)} %get-tuple-element.991) | copy-start | bytes 3076
  11.4 327.2 %copy-start.80 = (f32[256,1]{0,1:T(1,128)}, f32[256,1]{0,1:T(1,128)S(1)}, u32[]{:S(2)}) copy-start(f32[256,1]{0,1:T(1,128)S(1)} %get-tuple-element.992) | copy-start | bytes 3076
  11.4 327.2 %copy-start.82 = (f32[256,1]{0,1:T(1,128)}, f32[256,1]{0,1:T(1,128)S(1)}, u32[]{:S(2)}) copy-start(f32[256,1]{0,1:T(1,128)S(1)} %get-tuple-element.993) | copy-start | bytes 3076
  11.4 327.2 %copy-start.84 = (f32[256,1]{0,1:T(1,128)}, f32[256,1]{0,1:T(1,128)S(1)}, u32[]{:S(2)}) copy-start(f32[256,1]{0,1:T(1,128)S(1)} %get-tuple-element.994) | copy-start | bytes 3076
  11.6 222.6 %copy-start.12 = (bf16[2,64,2048]{2,1,0:T(8,128)(2,1)}, bf16[2,64,2048]{2,1,0:T(8,128)(2,1)S(1)}, u32[]{:S(2)}) copy-start(bf16[2,64,2048]{2,1,0:T(8,128)(2,1)S(1)} %fusion.138) | copy-start | bytes 1572868
  235.3 13.2 all-to-all-start
  239.6 112.6 %copy-start.65 = (f32[512,1]{0,1:T(1,128)}, f32[512,1]{0,1:T(1,128)S(1)}, u32[]{:S(2)}) copy-start(f32[512,1]{0,1:T(1,128)S(1)} %get-tuple-element.995) | copy-start | bytes 6148
  239.6 112.6 %copy-start.67 = (f32[512,1]{0,1:T(1,128)}, f32[512,1]{0,1:T(1,128)S(1)}, u32[]{:S(2)}) copy-start(f32[512,1]{0,1:T(1,128)S(1)} %get-tuple-element.996) | copy-start | bytes 6148
  239.7 112.6 %copy-start.69 = (f32[512,1]{0,1:T(1,128)}, f32[512,1]{0,1:T(1,128)S(1)}, u32[]{:S(2)}) copy-start(f32[512,1]{0,1:T(1,128)S(1)} %get-tuple-element.997) | copy-start | bytes 6148
  239.7 112.6 %copy-start.71 = (f32[512,1]{0,1:T(1,128)}, f32[512,1]{0,1:T(1,128)S(1)}, u32[]{:S(2)}) copy-start(f32[512,1]{0,1:T(1,128)S(1)} %get-tuple-element.998) | copy-start | bytes 6148
  248.5 90.1 %slice-start = ((f32[4352]{0:T(1024)}), f32[256]{0:T(256)S(1)}, s32[]{:S(2)}) async-start(f32[4352]{0:T(1024)} %param.20), calls=%async_computation.17 | async-start | bytes 2048 | tf_op jit(solution)/shard_map/slice | solution.py:158
  248.5 93.7 %all-to-all-start.1 = ((bf16[8,2,32768]{2,1,0:T(2,128)(2,1)}), bf16[8,2,32768]{2,1,0:T(2,128)(2,1)}, u32[]{:S(2)}, u32[]{:S(2)}) async-start(bf16[8,2,32768]{2,1,0:T(2,128)(2,1)} %reshape.630), calls=%async_computation.1 | async-start | bytes 2097152 | tf_op jit(solution)/shard_map/all_to_all | solution.py:141
  254.7 86.9 %copy-start.88 = (f32[8]{0:T(128)}, f32[8]{0:T(128)S(1)}, u32[]{:S(2)}) copy-start(f32[8]{0:T(128)S(1)} %fusion.165) | copy-start | bytes 100
  300.3 103.7 %copy-start.73 = (f32[512]{0:T(512)}, f32[512]{0:T(512)S(1)}, u32[]{:S(2)}) copy-start(f32[512]{0:T(512)S(1)} %mul.981) | copy-start | bytes 6148
  459.3 27.2 all-to-all-start.3
  463.7 261.9 %reduce-scatter.5.cloned.1.call-start = ((), (), s32[]{:S(2)}) async-start(), calls=%async_computation.12 | async-start | bytes 589824 | tf_op jit(solution)/shard_map/reduce_scatter | solution.py:199
  640.6 771.9 %reduce-scatter.7.cloned.1.call-start = ((), (), s32[]{:S(2)}) async-start(), calls=%async_computation.14 | async-start | bytes 34603008 | tf_op jit(solution)/shard_map/reduce_scatter | solution.py:227
  667.8 19.5 all-to-all-start.5
  687.2 38.0 %all-to-all-start.4 = ((bf16[2,512,512]{2,0,1:T(2,128)(2,1)}), bf16[2,512,512]{2,0,1:T(2,128)(2,1)S(1)}, u32[]{:S(2)}, u32[]{:S(2)}) async-start(bf16[2,512,512]{2,0,1:T(2,128)(2,1)} %copy.393), calls=%async_computation.4 | async-start | bytes 2097152 | tf_op jit(solution)/shard_map/all_to_all | solution.py:192
  693.2 1494.1 %reduce-scatter.9.cloned.1.call-start = ((), (), s32[]{:S(2)}) async-start(), calls=%async_computation.15 | async-start | bytes 37847040 | tf_op jit(solution)/shard_map/reduce_scatter | solution.py:227
  768.0 1544.1 %all-reduce.30.cloned.1.call-start = ((), (), s32[]{:S(2)}) async-start(), calls=%async_computation.13 | async-start | bytes 139264 | tf_op jit(solution)/shard_map/psum | solution.py:275
  783.3 2240.0 %reduce-scatter.11.cloned.1.call-start = ((), (), s32[]{:S(2)}) async-start(), calls=%async_computation.16 | async-start | bytes 34603008 | tf_op jit(solution)/shard_map/reduce_scatter | solution.py:239
  (115 other events, 928.9 us)
Sparse Core Ops, SparseCore 0:
  10.9 205.0 all-gather.3
  219.0 140.4 all-gather.5
  640.7 61.2 reduce-scatter.4
  704.3 708.2 reduce-scatter.6
  1414.8 772.4 reduce-scatter.8
  2194.3 117.8 all-reduce.29
  2315.1 708.1 reduce-scatter.10
where the time goes:
time: 3040 us; the launch traced here: 3030 us
  waiting for transfers between devices  2380 us (78%)
  matrix products  258 us (8%)
  blocking collectives  156 us (5%)
  local copies, waits for them, and re-layouts  127 us (4%)
  other arithmetic  75.3 us (2%)
    reduce_scatter x2, waiting for transfers between devices, shards(): lax.psum_scatter(in_term(jnp.int32(0), in_rows * lax.axis_size(('dp', 'se...  1300 us
    reduce_scatter x1, waiting for transfers between devices, shards(): lax.psum_scatter(out_term(jnp.int32(0), out_rows * lax.axis_size(('dp', '...  711 us
    all_gather x1, waiting for transfers between devices, shards(): lax.all_gather(in_weight, ('dp', 'seq'), axis=0, tiled=True)  204 us
    psum x1, waiting for transfers between devices, shards(): lax.psum((grad_conv_w, grad_conv_b, grad_shift, grad_decay, grad_skip, d_...  122 us
    dot_general x4, matrix products, in_term(): lax.dot_general(normed_one, d_one, (((0,), (0,)), ((), ())), preferred_el...  79.6 us
  transfers between devices with their start and end apart: 12, of which 7 were waited for; matrix products, arithmetic and copies ran while one was open for 9% of the time, Pallas kernels for 0%

commit v1 on v0

--- a/solution.py
+++ b/solution.py
@@ -111,7 +111,7 @@
     return mixed.reshape(length, head_count * HDIM)
 
 
-def shards(
+def general_plan(
     hidden,
     segments,
     in_weight,
@@ -291,7 +291,169 @@
     )
 
 
+def head_plan(
+    hidden,
+    segments,
+    in_weight,
+    conv_weight,
+    conv_bias,
+    dt_bias,
+    a_log,
+    d_skip,
+    norm_gain,
+    gate_gain,
+    out_weight,
+    cotangent,
+):
+    f32, bf16 = jnp.float32, jnp.bfloat16
+    n_dp, n_seq = lax.axis_size("dp"), lax.axis_size("seq")
+    seq_rank = lax.axis_index("seq")
+    n_own, shard_len, width = hidden.shape
+    length = shard_len * n_seq
+    rows = out_weight.shape[0]
+    in_rows = in_weight.shape[0]
+    chan = rows * n_dp
+    h_own = chan // HDIM
+    hidden_f = hidden.astype(f32)
+    inv = lax.rsqrt(jnp.mean(hidden_f * hidden_f, axis=-1, keepdims=True) + 1e-05)
+    normed = (hidden_f * inv * norm_gain).astype(bf16)
+    normed_all = lax.all_gather(normed, "seq", axis=1, tiled=True).reshape(n_own * length, width)
+    wide = in_weight[:, : 2 * DI].reshape(in_rows, 2, n_dp, n_seq, rows)
+    wide = lax.all_to_all(wide, "seq", split_axis=3, concat_axis=0, tiled=True)
+    wide = wide.reshape(n_seq * in_rows, 2 * chan)
+    tail = lax.all_gather(in_weight[:, 2 * DI :], "seq", axis=0, tiled=True)
+    w_in = lax.all_gather(jnp.concatenate([wide, tail], axis=1), "dp", axis=0, tiled=True)
+    w_out = lax.all_gather(out_weight, "dp", axis=0, tiled=True)
+    cot_all = lax.all_gather(cotangent, "seq", axis=1, tiled=True).reshape(n_own * length, width)
+    seg_all = lax.all_gather(segments, "seq", axis=1, tiled=True)
+
+    def own_chan(vec):
+        return lax.dynamic_index_in_dim(
+            vec.reshape((n_dp, n_seq, rows) + vec.shape[1:]), seq_rank, 1, keepdims=False
+        ).reshape((chan,) + vec.shape[1:])
+
+    heads_row = rows // HDIM
+
+    def own_head(vec):
+        return lax.dynamic_index_in_dim(
+            vec.reshape((n_dp, n_seq, heads_row) + vec.shape[1:]), seq_rank, 1, keepdims=False
+        ).reshape((h_own,) + vec.shape[1:])
+
+    def spread_chan(vec):
+        blank = jnp.zeros((n_dp, n_seq, rows) + vec.shape[1:], f32)
+        piece = vec.reshape((n_dp, 1, rows) + vec.shape[1:])
+        return lax.dynamic_update_slice_in_dim(blank, piece, seq_rank, 1).reshape(
+            (DI,) + vec.shape[1:]
+        )
+
+    def spread_head(vec):
+        blank = jnp.zeros((n_dp, n_seq, heads_row) + vec.shape[1:], f32)
+        piece = vec.reshape((n_dp, 1, heads_row) + vec.shape[1:])
+        return lax.dynamic_update_slice_in_dim(blank, piece, seq_rank, 1).reshape(
+            (HEADS,) + vec.shape[1:]
+        )
+
+    project = jnp.dot(normed_all, w_in, preferred_element_type=f32)
+    z = project[:, :chan]
+    x_raw = project[:, chan : 2 * chan].astype(bf16)
+    bc_raw = project[:, 2 * chan : 2 * chan + 2 * NST].astype(bf16)
+    dt_all = project[:, 2 * chan + 2 * NST :].astype(bf16)
+    dt_raw = own_head(dt_all.T).T
+    local_params = (
+        own_chan(conv_weight[:DI]),
+        own_chan(conv_bias[:DI]),
+        conv_weight[DI:],
+        conv_bias[DI:],
+        own_head(dt_bias),
+        own_head(a_log),
+        own_head(d_skip),
+    )
+
+    def head_mixer(x_values, step_raw, bc_values, params_in):
+        def single_seq(x_one, step_one, bc_one, seg_one):
+            return mixer(x_one, step_one, bc_one, seg_one, *params_in)
+
+        return jax.vmap(single_seq)(x_values, step_raw, bc_values, seg_all)
+
+    def by_seq(v):
+        return v.reshape(n_own, length, v.shape[-1]).astype(f32)
+
+    mixed, pull_mix = jax.vjp(
+        head_mixer, by_seq(x_raw), by_seq(dt_raw), by_seq(bc_raw), local_params
+    )
+    y = mixed.reshape(n_own * length, chan).astype(bf16).astype(f32)
+    gain = own_chan(gate_gain)
+    sig = jax.nn.sigmoid(z)
+    act = z * sig
+    g = y * act
+    d_gated = lax.dot_general(
+        cot_all, w_out, (((1,), (1,)), ((), ())), preferred_element_type=f32
+    )
+    u = d_gated * gain
+    sums = lax.psum(jnp.stack([jnp.sum(g * g, axis=1), jnp.sum(u * g, axis=1)]), "seq")
+    r = lax.rsqrt(sums[0] / DI + 1e-05)[:, None]
+    fall = (r * r * r) * (sums[1] / DI)[:, None]
+    gr = g * r
+    gated = (gr * gain).astype(bf16)
+    part = jnp.dot(gated, w_out, preferred_element_type=f32).astype(bf16)
+    branch = lax.psum_scatter(
+        part.reshape(n_own, length, width), "seq", scatter_dimension=1, tiled=True
+    )
+    result = (hidden_f + branch.astype(f32)).astype(bf16)
+    d_g = r * u - fall * g
+    d_y = (d_g * act).astype(bf16)
+    d_z = d_g * y * (sig * (1.0 + z * (1.0 - sig)))
+    d_gate_gain = jnp.sum(d_gated * gr, axis=0)
+    grad_out = jnp.einsum("tf,td->fd", gated, cot_all, preferred_element_type=f32)
+    grad_out = lax.psum_scatter(grad_out, "dp", scatter_dimension=0, tiled=True)
+    d_x, d_dt, d_bc, d_params = pull_mix(by_seq(d_y))
+    d_project = jnp.concatenate(
+        [
+            d_z,
+            d_x.reshape(n_own * length, chan),
+            d_bc.reshape(n_own * length, 2 * NST),
+            spread_head(d_dt.reshape(n_own * length, h_own).T).T,
+        ],
+        axis=1,
+    ).astype(bf16)
+    d_normed = lax.dot_general(
+        d_project, w_in, (((1,), (1,)), ((), ())), preferred_element_type=f32
+    ).astype(bf16)
+    d_normed = lax.psum_scatter(
+        d_normed.reshape(n_own, length, width), "seq", scatter_dimension=1, tiled=True
+    ).astype(f32)
+    grad_in = jnp.einsum("td,tf->df", normed_all, d_project, preferred_element_type=f32)
+    grad_in = lax.psum_scatter(grad_in, "dp", scatter_dimension=0, tiled=True)
+    grad_wide = grad_in[:, : 2 * chan].reshape(n_seq, in_rows, 2, n_dp, 1, rows)
+    grad_wide = lax.all_to_all(grad_wide, "seq", split_axis=0, concat_axis=4, tiled=True)
+    grad_wide = grad_wide.reshape(in_rows, 2 * DI)
+    grad_tail = lax.psum_scatter(grad_in[:, 2 * chan :], "seq", scatter_dimension=0, tiled=True)
+    grad_in = jnp.concatenate([grad_wide, grad_tail], axis=1)
+    dn = d_normed * norm_gain
+    along = jnp.mean(dn * hidden_f, axis=-1, keepdims=True)
+    d_hidden = (
+        cotangent.astype(f32) + inv * dn - (inv * inv * inv) * along * hidden_f
+    ).astype(bf16)
+    d_norm_gain = jnp.sum(d_normed * hidden_f * inv, axis=(0, 1))
+    d_kernel_x, d_offset_x, d_kernel_bc, d_offset_bc, d_shift, d_decay, d_skip_part = d_params
+    totals = lax.psum(
+        (
+            jnp.concatenate([spread_chan(d_kernel_x), d_kernel_bc], axis=0),
+            jnp.concatenate([spread_chan(d_offset_x), d_offset_bc], axis=0),
+            spread_head(d_shift),
+            spread_head(d_decay),
+            spread_head(d_skip_part),
+            d_norm_gain,
+            spread_chan(d_gate_gain),
+        ),
+        ("dp", "seq"),
+    )
+    return (result, d_hidden, grad_in) + tuple(totals) + (grad_out,)
+
+
 def solution(mesh):
+    whole_heads = (DI // mesh.size) % HDIM == 0
+    shards = head_plan if whole_heads else general_plan
     placed = (
         P("dp", "seq", None),
         P("dp", "seq"),

time: 3040 us -> 1010 us (0.33)
  waiting for transfers between devices: 2380 us -> 511 us
  matrix products: 258 us -> 141 us
  local copies, waits for them, and re-layouts: 127 us -> 94.7 us
    reduce_scatter x4 -> x5, waiting for transfers between devices: 2010 us -> 319 us  [the longest x1 95.9 us: head_plan(): lax.psum_scatter(d_normed.reshape(n_own, length, width), 'seq', scatter_d...]
    all_gather x2 -> x4, waiting for transfers between devices: 204 us -> 69.3 us  [the longest x1 44 us: head_plan(): lax.all_gather(jnp.concatenate([wide, tail], axis=1), 'dp', axis=0, tiled...]
    dot_general x10 -> x6, matrix products: 176 us -> 59.3 us  [the longest x1 14.4 us: head_plan(): jnp.einsum('td,tf->df', normed_all, d_project, preferred_element_type=f32)]
    all_to_all x5 -> x2, waiting for transfers between devices: 40.8 us -> 0.01 us  [the longest x1 0.01 us: head_plan(): lax.all_to_all(grad_wide, 'seq', split_axis=0, concat_axis=4, tiled=True)]
    psum x1 -> x2, blocking collectives: 53.5 us -> 62.7 us  [the longest x1 43.7 us: head_plan(): lax.psum((jnp.concatenate([spread_chan(d_kernel_x), d_kernel_bc], axis=0)...]
  transfers between devices with their start and end apart: 12 -> 12, of which waited for: 7 -> 8; matrix products, arithmetic and copies ran while one was open for 9% -> 12% of each run, Pallas kernels for 0% -> 0%
where the time goes in v1:
time: 1010 us; the launch traced here: 999 us
  waiting for transfers between devices  511 us (51%)
  blocking collectives  146 us (14%)
  matrix products  141 us (14%)
  local copies, waits for them, and re-layouts  94.7 us (9%)
  other arithmetic  74.8 us (7%)
  between operations  15.5 us (2%)
  starting transfers between devices  13.6 us (1%)
    psum x1, waiting for transfers between devices, head_plan(): lax.psum((jnp.concatenate([spread_chan(d_kernel_x), d_kernel_bc], axis=0)...  122 us
    reduce_scatter x1, waiting for transfers between devices, head_plan(): lax.psum_scatter(d_normed.reshape(n_own, length, width), 'seq', scatter_d...  95.9 us
    reduce_scatter x1, waiting for transfers between devices, head_plan(): grad_in = lax.psum_scatter(grad_in, 'dp', scatter_dimension=0, tiled=True)  66.5 us
    all_gather x1, blocking collectives, head_plan(): tail = lax.all_gather(in_weight[:, 2 * DI:], 'seq', axis=0, tiled=True)  64.1 us
    reduce_scatter x1, waiting for transfers between devices, head_plan(): lax.psum_scatter(grad_in[:, 2 * chan:], 'seq', scatter_dimension=0, tiled...  58.6 us
    reduce_scatter x1, waiting for transfers between devices, head_plan(): grad_out = lax.psum_scatter(grad_out, 'dp', scatter_dimension=0, tiled=True)  49.9 us
    reduce_scatter x1, waiting for transfers between devices, head_plan(): lax.psum_scatter(part.reshape(n_own, length, width), 'seq', scatter_dimen...  47.7 us
    all_gather x1, waiting for transfers between devices, head_plan(): lax.all_gather(jnp.concatenate([wide, tail], axis=1), 'dp', axis=0, tiled...  44 us
  transfers between devices with their start and end apart: 12, of which 8 were waited for; matrix products, arithmetic and copies ran while one was open for 12% of the time, Pallas kernels for 0%

profile of v1, /device:TPU:0, one launch (start us, length us, event | category | flops | bytes accessed | tf_op | source)
XLA Modules:
  0.0 998.7 jit_solution(3665931072201139039)
XLA Ops:
  12.4 7.3 all-to-all-start
  19.7 64.1 %all_gather.19 = bf16[512,320]{1,0:T(8,128)(2,1)S(1)} all-gather(bf16[64,320]{1,0:T(8,128)(2,1)S(1)} %slice-done.1), channel_id=1, replica_groups=mesh['dp'=4,'seq'=8] {'seq'}, dimensions={0}, use_global_device_ids=true | all-gather | bytes 368640 | tf_op jit(solution)/shard_map/all_gather | solution.py:324
  87.3 19.6 %all-gather = s32[8,64,2]{1,2,0:T(2,128)S(1)} all-gather(s32[1,64,2]{1,2,0:T(2,128)S(1)} %bitcast.576), channel_id=1, replica_groups=mesh['dp'=4,'seq'=8] {'seq'}, dimensions={0}, use_global_device_ids=true | all-gather | bytes 4608 | tf_op jit(solution)/shard_map/all_gather | solution.py:328
  110.1 44.0 %all-gather.8.cloned.1.call-done = bf16[2048,1344]{1,0:T(8,128)(2,1)} async-done(((bf16[512,1344]{1,0:T(8,128)(2,1)}), bf16[2048,1344]{1,0:T(8,128)(2,1)}) %all-gather.8.cloned.1.call-update) | async-done | bytes 5505040 | tf_op jit(solution)/shard_map/all_gather | solution.py:325
  154.1 11.0 %fusion.160 = (bf16[1024,1344]{0,1:T(8,128)(2,1)S(1)}, f32[1024,1344]{0,1:T(8,128)}) fusion(bf16[1024,2048]{1,0:T(8,128)(2,1)} %bitcast.579, bf16[2048,1344]{1,0:T(8,128)(2,1)} %all-gather.8.cloned.1.call-done), kind=kOutput, calls=%fused_computation.306 | convolution fusion | flops 5638520832 | bytes 17956864 | tf_op jit(solution)/shard_map/dot_general | solution.py:356
  185.0 33.3 %while.46 = (s32[]{:T(128)}, f32[2,8,64,128]{3,2,1,0:T(8,128)S(1)}, s32[2]{0:T(128)S(1)}, f32[2,2,256,8,64]{2,4,3,1,0:T(8,128)}, f32[2,2,8,64,128]{4,3,2,1,0:T(8...) while((s32[]{:T(128)}, f32[2,8,64,128]{3,2,1,0:T(8,128)S(1)}, ...), condition=%wide.region_4.5_spmd.clone, body=%wide.region_1.4_spmd.clone.sunk | while | flops 1819494400 | bytes 10638929 | solution.py:83
  205.8 6.2 fusion.228
  228.5 25.3 %all-gather.10.cloned.1.call-done = bf16[2,512,2048]{2,1,0:T(8,128)(2,1)} async-done(((bf16[2,64,2048]{2,1,0:T(8,128)(2,1)}), bf16[2,512,2048]{2,1,0:T(8,128)(2,1)}) %all-gather.10.cloned.1.call-update) | async-done | bytes 4194320 | tf_op jit(solution)/shard_map/all_gather | solution.py:327
  253.8 9.9 multiply_reduce_fusion.10
  263.7 19.0 %psum.56 = f32[2,1024]{1,0:T(2,128)S(1)} all-reduce(f32[2,1024]{1,0:T(2,128)S(1)} %pad_maximum_fusion.7), channel_id=1, replica_groups=mesh['dp'=4,'seq'=8] {'seq'}, use_global_device_ids=true, to_apply=%region_7.8 | all-reduce | flops 2048 | bytes 16384 | tf_op jit(solution)/shard_map/psum | solution.py:393
  298.6 116.2 %while.47 = (s32[]{:T(128)}, f32[2,8,64,128]{3,2,1,0:T(8,128)}, f32[2,2,256,8,64]{2,4,3,1,0:T(8,128)}, f32[2,2,256,8]{2,3,0,1:T(8,128)}, f32[2,2,256,8]{2,3,0,1:...) while((s32[]{:T(128)}, f32[2,8,64,128]{3,2,1,0:T(8,128)}, ...), condition=%wide.region_21.22_spmd.clone, body=%wide.region_9.21_spmd.clone.sunk | while | flops 4253304832 | bytes 55387352 | solution.py:83
  321.7 8.6 fusion.250
  380.1 8.6 fusion.250
  435.5 14.4 %fusion.130 = f32[2048,1344]{0,1:T(8,128)} fusion(bf16[1024,2048]{1,0:T(8,128)(2,1)} %bitcast.580, bf16[1024,64]{0,1:T(8,128)(2,1)S(1)} %bitcast.523, bf16[1024,256]{0,1:T(8,128)(2,1)S(1)} %copy.407, bf16[1024,512]{0,1:T(8,128)(2,1)S(1)} %bitcast.515, bf16[1024,512]{0,1:T(8,128)(2,1)S(1)} %copy-done.38), kind=kOutput, calls=%fused_computation.236 | convolution fusion | flops 5648154624 | bytes 17956864 | tf_op jit(solution)/shard_map/td,tf->df/dot_general | solution.py:425
  450.0 11.1 %convolution_convert_fusion = bf16[1024,2048]{1,0:T(8,128)(2,1)} fusion(bf16[2048,1344]{1,0:T(8,128)(2,1)} %all-gather.8.cloned.1.call-done, bf16[1024,64]{0,1:T(8,128)(2,1)S(1)} %bitcast.524, bf16[1024,256]{0,1:T(8,128)(2,1)S(1)} %copy.407, bf16[1024,512]{0,1:T(8,128)(2,1)S(1)} %bitcast.516, bf16[1024,512]{0,1:T(8,128)(2,1)S(1)} %copy-done.38), kind=kOutput, calls=%fused_computation.143 | convolution fusion | flops 5650251776 | bytes 12451840 | tf_op jit(solution)/shard_map/dot_general | solution.py:419
  463.1 6.3 convolution_convert_fusion.1
  469.5 66.5 %reduce-scatter.12.cloned.1.call-done = f32[512,1344]{0,1:T(8,128)} async-done(((f32[2048,1344]{0,1:T(8,128)}), f32[512,1344]{0,1:T(8,128)}) %reduce-scatter.12.cloned.1.call-update) | async-done | bytes 2752528 | tf_op jit(solution)/shard_map/reduce_scatter | solution.py:426
  539.5 6.6 fusion.153
  561.9 95.9 %reduce-scatter.10.cloned.1.call-done = bf16[2,64,2048]{2,1,0:T(8,128)(2,1)} async-done(((bf16[2,512,2048]{2,1,0:T(8,128)(2,1)}), bf16[2,64,2048]{2,1,0:T(8,128)(2,1)}) %reduce-scatter.10.cloned.1.call-update) | async-done | bytes 524304 | tf_op jit(solution)/shard_map/reduce_scatter | solution.py:422
  659.2 43.7 %all-reduce.27 = (f32[4352]{0:T(1024)}, f32[64]{0:T(128)}, f32[64]{0:T(128)}, f32[64]{0:T(128)}, f32[2048]{0:T(1024)}, /*index=5*/f32[4096]{0:T(1024)}) all-reduce(f32[4352]{0:T(1024)S(1)} %pad_maximum_fusion.6, f32[64]{0:T(128)S(1)} %reshape.753, f32[64]{0:T(128)S(1)} %reshape.754, ...), channel_id=1, replica_groups=mesh['dp'=4,'seq'=8] {'dp','seq'}, use_global_device_ids=true, to_apply=%region_37.38 | all-reduce | flops 10688 | bytes 85504 | tf_op jit(solution)/shard_map/psum | solution.py:439
  702.9 47.7 %reduce-scatter.8.cloned.1.call-done = bf16[2,64,2048]{2,1,0:T(8,128)(2,1)} async-done(((bf16[2,512,2048]{2,1,0:T(8,128)(2,1)}), bf16[2,64,2048]{2,1,0:T(8,128)(2,1)}) %reduce-scatter.8.cloned.1.call-update) | async-done | bytes 524304 | tf_op jit(solution)/shard_map/reduce_scatter | solution.py:399
  757.6 58.6 %reduce-scatter.16.cloned.1.call-done = f32[64,320]{1,0:T(8,128)} async-done(((f32[512,320]{1,0:T(8,128)}), f32[64,320]{1,0:T(8,128)}) %reduce-scatter.16.cloned.1.call-update) | async-done | bytes 81936 | tf_op jit(solution)/shard_map/reduce_scatter | solution.py:430
  818.6 121.6 %all-reduce.30.cloned.1.call-done = f32[4352,4]{0,1:T(4,128)} async-done(((f32[4352,4]{0,1:T(4,128)}), f32[4352,4]{0,1:T(4,128)}) %all-reduce.30.cloned.1.call-update) | async-done | bytes 69648 | tf_op jit(solution)/shard_map/psum | solution.py:439
  940.2 49.9 %reduce-scatter.14.cloned.1.call-done = f32[128,2048]{1,0:T(8,128)} async-done(((f32[512,2048]{1,0:T(8,128)}), f32[128,2048]{1,0:T(8,128)}) %reduce-scatter.14.cloned.1.call-update) | async-done | bytes 1048592 | tf_op jit(solution)/shard_map/reduce_scatter | solution.py:408
  (546 shorter events, 235.6 us)
Async XLA Ops:
  7.2 102.9 %copy-start = (f32[4096]{0:T(1024)S(1)}, f32[4096]{0:T(1024)}, u32[]{:S(2)}) copy-start(f32[4096]{0:T(1024)} %param.25) | copy-start | bytes 49156
  7.2 102.9 %all-gather.6.cloned.1.call-start = ((), (), s32[]{:S(2)}) async-start(), calls=%async_computation.7 | async-start | bytes 4718592 | tf_op jit(solution)/shard_map/all_gather | solution.py:320
  12.4 71.4 %all-to-all-start = ((bf16[64,2,4,8,128]{4,2,1,0,3:T(4,128)(2,1)}), bf16[64,2,4,8,128]{4,2,1,0,3:T(4,128)(2,1)S(1)}, u32[]{:S(2)}, u32[]{:S(2)}) async-start(bf16[64,2,4,8,128]{4,2,1,0,3:T(4,128)(2,1)} %copy.346), calls=%async_computation | async-start | bytes 2097152 | tf_op jit(solution)/shard_map/all_to_all | solution.py:322
  19.7 134.4 %all-gather.8.cloned.1.call-start = ((), (), s32[]{:S(2)}) async-start(), calls=%async_computation.8 | async-start | bytes 7208960 | tf_op jit(solution)/shard_map/all_gather | solution.py:325
  85.8 142.6 %all-gather.12.cloned.1.call-start = ((), (), s32[]{:S(2)}) async-start(), calls=%async_computation.10 | async-start | bytes 2621440 | tf_op jit(solution)/shard_map/all_gather | solution.py:326
  86.6 167.2 %all-gather.10.cloned.1.call-start = ((), (), s32[]{:S(2)}) async-start(), calls=%async_computation.9 | async-start | bytes 4718592 | tf_op jit(solution)/shard_map/all_gather | solution.py:327
  87.2 448.9 %reduce-scatter.12.cloned.1.call-start = ((), (), s32[]{:S(2)}) async-start(), calls=%async_computation.13 | async-start | bytes 13762560 | tf_op jit(solution)/shard_map/reduce_scatter | solution.py:426
  87.3 92.7 %copy-start.73 = (f32[256,1]{0,1:T(1,128)}, f32[256,1]{0,1:T(1,128)S(1)}, u32[]{:S(2)}) copy-start(f32[256,1]{0,1:T(1,128)S(1)} %get-tuple-element.962) | copy-start | bytes 3076
  87.3 92.7 %copy-start.75 = (f32[256,1]{0,1:T(1,128)}, f32[256,1]{0,1:T(1,128)S(1)}, u32[]{:S(2)}) copy-start(f32[256,1]{0,1:T(1,128)S(1)} %get-tuple-element.963) | copy-start | bytes 3076
  87.3 92.7 %copy-start.77 = (f32[256,1]{0,1:T(1,128)}, f32[256,1]{0,1:T(1,128)S(1)}, u32[]{:S(2)}) copy-start(f32[256,1]{0,1:T(1,128)S(1)} %get-tuple-element.964) | copy-start | bytes 3076
  110.1 143.7 %copy-start.87 = (f32[512]{0:T(512)}, f32[512]{0:T(512)S(1)}, u32[]{:S(2)}) copy-start(f32[512]{0:T(512)S(1)} %mul.1005) | copy-start | bytes 6148
  110.1 172.6 %copy-start.89 = (f32[4,1,128]{2,1,0:T(1,128)}, f32[4,1,128]{2,1,0:T(1,128)S(1)}, u32[]{:S(2)}) copy-start(f32[4,1,128]{2,1,0:T(1,128)S(1)} %constant_dynamic-slice_fusion.1) | copy-start | bytes 6148
  450.0 207.8 %reduce-scatter.10.cloned.1.call-start = ((), (), s32[]{:S(2)}) async-start(), calls=%async_computation.12 | async-start | bytes 4718592 | tf_op jit(solution)/shard_map/reduce_scatter | solution.py:422
  461.2 289.5 %reduce-scatter.8.cloned.1.call-start = ((), (), s32[]{:S(2)}) async-start(), calls=%async_computation.11 | async-start | bytes 4718592 | tf_op jit(solution)/shard_map/reduce_scatter | solution.py:399
  469.5 346.7 %reduce-scatter.16.cloned.1.call-start = ((), (), s32[]{:S(2)}) async-start(), calls=%async_computation.16 | async-start | bytes 884736 | tf_op jit(solution)/shard_map/reduce_scatter | solution.py:430
  538.4 401.8 %all-reduce.30.cloned.1.call-start = ((), (), s32[]{:S(2)}) async-start(), calls=%async_computation.14 | async-start | bytes 139264 | tf_op jit(solution)/shard_map/psum | solution.py:439
  539.3 450.8 %reduce-scatter.14.cloned.1.call-start = ((), (), s32[]{:S(2)}) async-start(), calls=%async_computation.15 | async-start | bytes 5242880 | tf_op jit(solution)/shard_map/reduce_scatter | solution.py:408
  554.1 103.7 %copy-start.15 = (bf16[2,64,2048]{2,1,0:T(8,128)(2,1)S(1)}, bf16[2,64,2048]{2,1,0:T(8,128)(2,1)}, u32[]{:S(2)}) copy-start(bf16[2,64,2048]{2,1,0:T(8,128)(2,1)} %param.16) | copy-start | bytes 1572868
  554.1 103.7 %copy-start.54 = (f32[2048]{0:T(1024)S(1)}, f32[2048]{0:T(1024)}, u32[]{:S(2)}) copy-start(f32[2048]{0:T(1024)} %param.24) | copy-start | bytes 24580
  554.1 103.7 %copy-start.69 = (f32[2,64]{1,0:T(2,128)S(1)}, f32[2,64]{1,0:T(2,128)}, u32[]{:S(2)}) copy-start(f32[2,64]{1,0:T(2,128)} %copy-done.68) | copy-start | bytes 1540
  554.1 148.8 %copy-start.82 = (f32[2,64]{1,0:T(2,128)S(1)}, f32[2,64]{1,0:T(2,128)}, u32[]{:S(2)}) copy-start(f32[2,64]{1,0:T(2,128)} %copy-done.81) | copy-start | bytes 1540
  554.1 196.5 %copy-start.31 = (bf16[2,64,2048]{2,1,0:T(8,128)(2,1)S(1)}, bf16[2,64,2048]{2,1,0:T(8,128)(2,1)}, u32[]{:S(2)}) copy-start(bf16[2,64,2048]{2,1,0:T(8,128)(2,1)} %param.27) | copy-start | bytes 1572868
  554.1 199.2 %all-to-all-start.1 = ((f32[8,64,2,4,1,128]{5,3,2,1,4,0:T(4,128)}), f32[8,64,2,4,1,128]{5,3,2,1,4,0:T(4,128)S(1)}, u32[]{:S(2)}, u32[]{:S(2)}) async-start(f32[8,64,2,4,1,128]{5,3,2,1,4,0:T(4,128)} %copy.382), calls=%async_computation.4 | async-start | bytes 4194304 | tf_op jit(solution)/shard_map/all_to_all | solution.py:428
  755.8 235.8 %copy-start.1 = (f32[4096]{0:T(1024)S(1)}, f32[4096]{0:T(1024)}, u32[]{:S(2)}) copy-start(f32[4096]{0:T(1024)} %param.25) | copy-start | bytes 49156
  (120 other events, 1265.6 us)
Sparse Core Ops, SparseCore 0:
  10.8 98.8 all-gather.5
  111.8 42.1 all-gather.7
  155.7 22.5 all-gather.11
  180.3 73.4 all-gather.9
  450.1 85.9 reduce-scatter.11
  539.5 118.2 reduce-scatter.9
  661.9 88.7 reduce-scatter.7
  753.9 62.2 reduce-scatter.15
  823.3 116.8 all-reduce.29
  943.3 46.7 reduce-scatter.13

commit v2 on v1

--- a/solution.py
+++ b/solution.py
@@ -1,12 +1,17 @@
+import functools
+
 import jax
 import jax.numpy as jnp
 from jax import lax
+from jax.experimental import pallas as pl
+from jax.experimental.pallas import tpu as pltpu
 from jax.sharding import PartitionSpec as P
 
 HEADS = 64
 HDIM = 64
 NST = 128
 GROUP = 256
+CONV = 4
 DI = 4096
 
 
@@ -289,6 +294,306 @@
         totals[6],
         grad_out,
     )
+
+
+LOG2E = 1.4426950408889634
+TILE = 128
+FAR = -1e30
+
+
+def shift_rows(v, lag):
+    return v if lag == 0 else pltpu.roll(v, lag % v.shape[0], axis=0)
+
+
+def conv_silu(sig, taps, offset, keep):
+    total = offset + taps[CONV - 1 : CONV] * sig
+    for lag in range(1, CONV):
+        total = total + taps[CONV - 1 - lag : CONV - lag] * (shift_rows(sig, lag) * keep[lag])
+    gate = jax.nn.sigmoid(total)
+    return total, gate, total * gate
+
+
+def conv_back(d_out, total, gate, sig, taps, keep):
+    d_total = d_out * (gate * (1.0 + total * (1.0 - gate)))
+    d_sig = taps[CONV - 1 : CONV] * d_total
+    tap_rows = [jnp.sum(d_total * sig, axis=0, keepdims=True)]
+    for lag in range(1, CONV):
+        kept = d_total * keep[lag]
+        d_sig = d_sig + taps[CONV - 1 - lag : CONV - lag] * shift_rows(kept, -lag)
+        tap_rows.append(jnp.sum(kept * shift_rows(sig, lag), axis=0, keepdims=True))
+    return d_sig, tap_rows[::-1], jnp.sum(d_total, axis=0, keepdims=True)
+
+
+def keep_masks(seg_col):
+    length = seg_col.shape[0]
+    row = lax.broadcasted_iota(jnp.int32, (length, 1), 0)
+    masks = [None]
+    for lag in range(1, CONV):
+        same = (pltpu.roll(seg_col, lag, axis=0) == seg_col) & (row >= lag)
+        masks.append(same.astype(jnp.float32))
+    return masks
+
+
+def lane_sums(v, reverse):
+    length = v.shape[1]
+    lane = lax.broadcasted_iota(jnp.int32, v.shape, 1)
+    step = 1
+    while step < length:
+        if reverse:
+            v = v + jnp.where(lane < length - step, pltpu.roll(v, length - step, axis=1), 0.0)
+        else:
+            v = v + jnp.where(lane >= step, pltpu.roll(v, step, axis=1), 0.0)
+        step *= 2
+    return v
+
+
+def step_sizes_of(dt_all, head_rows, h_own, n_seq, heads_row):
+    rank = lax.axis_index("seq")
+    all_heads = dt_all.shape[1]
+    lane = lax.broadcasted_iota(jnp.int32, (all_heads, 128), 1)
+    row = lax.broadcasted_iota(jnp.int32, (all_heads, 128), 0)
+    head = ((lane // heads_row) * n_seq + rank) * heads_row + lane % heads_row
+    pick = ((row == head) & (lane < h_own)).astype(jnp.bfloat16)
+    raw = jnp.dot(dt_all, pick, preferred_element_type=jnp.float32)
+    shifted = raw + head_rows[0:1]
+    dt = jnp.maximum(shifted, 0.0) + jnp.log1p(jnp.exp(-jnp.abs(shifted)))
+    return shifted, dt
+
+
+def head_prep(dt_all, head_rows, h_own, n_seq, heads_row, dt_cols, cum_cols, cum_rows):
+    shifted, dt = step_sizes_of(dt_all, head_rows, h_own, n_seq, heads_row)
+    rates = -jnp.exp(head_rows[1:2])
+    step_log = dt * (rates * LOG2E)
+    across = jnp.transpose(step_log)
+    cum_t = lane_sums(across[:h_own], False)
+    pad = jnp.zeros((128 - h_own, cum_t.shape[1]), jnp.float32)
+    cum = jnp.transpose(jnp.concatenate([cum_t, pad], axis=0))
+    for k in range(h_own):
+        dt_cols[k] = dt[:, k : k + 1]
+        cum_cols[k] = cum[:, k : k + 1]
+        cum_rows[k] = cum_t[k : k + 1, :]
+    return shifted, dt
+
+
+def pair_wide(cols, pair):
+    length = cols.shape[1]
+    lane = lax.broadcasted_iota(jnp.int32, (length, 128), 1)
+    return jnp.where(lane < HDIM, cols[2 * pair], cols[2 * pair + 1])
+
+
+def scan_forward(h_own, n_seq, heads_row, x_ref, bc_ref, dt_ref, segc_ref, segr_ref, wx_ref, wbc_ref,
+                 head_ref, y_ref, inner_ref, dt_cols, cum_cols, cum_rows, inner_prod, bias):
+    pair = pl.program_id(1)
+    length = x_ref.shape[0]
+    seg_col = segc_ref[0]
+    keep = keep_masks(seg_col)
+
+    @pl.when(pair == 0)
+    def prepare():
+        head_prep(dt_ref[...], head_ref[...], h_own, n_seq, heads_row, dt_cols, cum_cols, cum_rows)
+        _, _, bc = conv_silu(bc_ref[...].astype(jnp.float32), wbc_ref[0:CONV], wbc_ref[CONV : CONV + 1], keep)
+        inner_prod[...] = lax.dot_general(
+            bc[:, NST:], bc[:, :NST], (((1,), (1,)), ((), ())),
+            precision=lax.Precision.HIGHEST, preferred_element_type=jnp.float32,
+        )
+        at = lax.broadcasted_iota(jnp.int32, (length, length), 0)
+        source = lax.broadcasted_iota(jnp.int32, (length, length), 1)
+        bias[...] = jnp.where((source <= at) & (seg_col == segr_ref[0]), 0.0, FAR)
+
+    _, _, xc = conv_silu(x_ref[...].astype(jnp.float32), wx_ref[0:CONV], wx_ref[CONV : CONV + 1], keep)
+    moved = (xc * pair_wide(dt_cols, pair)).astype(jnp.bfloat16)
+    skip = wx_ref[CONV + 1 : CONV + 2]
+    first = lax.broadcasted_iota(jnp.int32, (TILE, 128), 1) < HDIM
+    for block in range(length // TILE):
+        rows, wide = slice(block * TILE, (block + 1) * TILE), (block + 1) * TILE
+        halves = []
+        for half in range(2):
+            head = 2 * pair + half
+            decay = jnp.exp2(cum_cols[head, rows] - cum_rows[head, :, :wide] + bias[rows, :wide])
+            scores = (inner_prod[rows, :wide] * decay).astype(jnp.bfloat16)
+            halves.append(jnp.dot(scores, moved[:wide], preferred_element_type=jnp.float32))
+        inner = jnp.where(first, halves[0], halves[1])
+        inner_ref[rows] = inner
+        y_ref[rows] = (inner + skip * xc[rows]).astype(jnp.bfloat16)
+
+
+def scan_backward(h_own, n_seq, heads_row, x_ref, bc_ref, dt_ref, segc_ref, segr_ref, wx_ref, wbc_ref,
+                  head_ref, dy_ref, inner_ref, dx_ref, dbc_ref, ddt_ref, gx_ref, gbc_ref, gh_ref,
+                  dt_cols, cum_cols, cum_rows, inner_prod, bias, d_inner, d_cum, d_dt):
+    pair = pl.program_id(1)
+    n_pair = pl.num_programs(1)
+    length = x_ref.shape[0]
+    seg_col = segc_ref[0]
+    keep = keep_masks(seg_col)
+    f32, bf16 = jnp.float32, jnp.bfloat16
+
+    @pl.when(pair == 0)
+    def prepare():
+        head_prep(dt_ref[...], head_ref[...], h_own, n_seq, heads_row, dt_cols, cum_cols, cum_rows)
+        _, _, bc = conv_silu(bc_ref[...].astype(f32), wbc_ref[0:CONV], wbc_ref[CONV : CONV + 1], keep)
+        inner_prod[...] = lax.dot_general(
+            bc[:, :NST], bc[:, NST:], (((1,), (1,)), ((), ())),
+            precision=lax.Precision.HIGHEST, preferred_element_type=f32,
+        )
+        source = lax.broadcasted_iota(jnp.int32, (length, length), 0)
+        at = lax.broadcasted_iota(jnp.int32, (length, length), 1)
+        bias[...] = jnp.where((source <= at) & (seg_col == segr_ref[0]), 0.0, FAR)
+        d_inner[...] = jnp.zeros((length, length), f32)
+        d_cum[...] = jnp.zeros((length, 128), f32)
+        d_dt[...] = jnp.zeros((length, 128), f32)
+
+    x_in = x_ref[...].astype(f32)
+    taps = wx_ref[0:CONV]
+    total, gate, xc = conv_silu(x_in, taps, wx_ref[CONV : CONV + 1], keep)
+    dt_wide = pair_wide(dt_cols, pair)
+    moved = (xc * dt_wide).astype(bf16)
+    skip = wx_ref[CONV + 1 : CONV + 2]
+    dy = dy_ref[...]
+    first = lax.broadcasted_iota(jnp.int32, (TILE, 128), 1) < HDIM
+    pieces = []
+    for block in range(length // TILE):
+        rows, later = slice(block * TILE, (block + 1) * TILE), slice(block * TILE, length)
+        halves = []
+        for half in range(2):
+            head = 2 * pair + half
+            decay = jnp.exp2(cum_rows[head, :, later] - cum_cols[head, rows] + bias[rows, later])
+            scores = (inner_prod[rows, later] * decay).astype(bf16)
+            halves.append(jnp.dot(scores, dy[later], preferred_element_type=f32))
+            mine = jnp.where(first if half == 0 else ~first, moved[rows].astype(f32), 0.0).astype(bf16)
+            d_scores = lax.dot_general(
+                mine, dy[later], (((1,), (1,)), ((), ())), preferred_element_type=f32
+            )
+            d_inner[rows, later] += d_scores * decay
+        pieces.append(jnp.where(first, halves[0], halves[1]))
+    d_moved = jnp.concatenate(pieces, axis=0)
+    dy_f = dy.astype(f32)
+    change = dy_f * inner_ref[...] - moved.astype(f32) * d_moved
+    direct = d_moved * xc
+    lane = lax.broadcasted_iota(jnp.int32, (length, 128), 1)
+    low = lane < HDIM
+    for half in range(2):
+        mine = low if half == 0 else ~low
+        place = lane == 2 * pair + half
+        d_cum[...] += jnp.where(place, jnp.sum(jnp.where(mine, change, 0.0), axis=1, keepdims=True), 0.0)
+        d_dt[...] += jnp.where(place, jnp.sum(jnp.where(mine, direct, 0.0), axis=1, keepdims=True), 0.0)
+    d_xc = d_moved * dt_wide + skip * dy_f
+    d_x, tap_rows, d_offset = conv_back(d_xc, total, gate, x_in, taps, keep)
+    dx_ref[...] = d_x.astype(bf16)
+    d_skip = jnp.sum(dy_f * xc, axis=0, keepdims=True)
+    blank = jnp.zeros((2, 128), f32)
+    gx_ref[0] = jnp.concatenate(tap_rows + [d_offset, d_skip, blank], axis=0)
+
+    @pl.when(pair == n_pair - 1)
+    def finish():
+        bc_in = bc_ref[...].astype(f32)
+        taps_bc = wbc_ref[0:CONV]
+        total_bc, gate_bc, bc = conv_silu(bc_in, taps_bc, wbc_ref[CONV : CONV + 1], keep)
+        d_in = d_inner[...]
+        d_b = jnp.dot(d_in, bc[:, NST:], precision=lax.Precision.HIGHEST, preferred_element_type=f32)
+        d_c = lax.dot_general(
+            d_in, bc[:, :NST], (((0,), (0,)), ((), ())),
+            precision=lax.Precision.HIGHEST, preferred_element_type=f32,
+        )
+        d_bc, rows_bc, offset_bc = conv_back(
+            jnp.concatenate([d_b, d_c], axis=1), total_bc, gate_bc, bc_in, taps_bc, keep
+        )
+        dbc_ref[...] = d_bc.astype(bf16)
+        gbc_ref[0] = jnp.concatenate(rows_bc + [offset_bc, jnp.zeros((3, 2 * NST), f32)], axis=0)
+        shifted, dt = step_sizes_of(dt_ref[...], head_ref[...], h_own, n_seq, heads_row)
+        rates = -jnp.exp(head_ref[1:2])
+        across = jnp.transpose(d_cum[...])
+        d_log_t = lane_sums(across[:h_own], True)
+        pad = jnp.zeros((128 - h_own, length), f32)
+        d_log = jnp.transpose(jnp.concatenate([d_log_t, pad], axis=0))
+        d_raw = (d_log * rates + d_dt[...]) * jax.nn.sigmoid(shifted)
+        ddt_ref[...] = d_raw
+        gh_ref[0] = jnp.concatenate(
+            [
+                jnp.sum(d_raw, axis=0, keepdims=True),
+                jnp.sum(d_log * dt, axis=0, keepdims=True) * rates,
+                jnp.zeros((6, 128), f32),
+            ],
+            axis=0,
+        )
+
+
+def scan_specs(length, all_heads):
+    return [
+        pl.BlockSpec((length, 128), lambda q, p: (q, p)),
+        pl.BlockSpec((length, 2 * NST), lambda q, p: (q, 0)),
+        pl.BlockSpec((length, all_heads), lambda q, p: (q, 0)),
+        pl.BlockSpec((1, length, 1), lambda q, p: (q, 0, 0)),
+        pl.BlockSpec((1, 1, length), lambda q, p: (q, 0, 0)),
+        pl.BlockSpec((8, 128), lambda q, p: (0, p)),
+        pl.BlockSpec((8, 2 * NST), lambda q, p: (0, 0)),
+        pl.BlockSpec((8, 128), lambda q, p: (0, 0)),
+    ]
+
+
+def scan_scratch(length, h_own):
+    f32 = jnp.float32
+    return [
+        pltpu.VMEM((h_own, length, 1), f32),
+        pltpu.VMEM((h_own, length, 1), f32),
+        pltpu.VMEM((h_own, 1, length), f32),
+        pltpu.VMEM((length, length), f32),
+        pltpu.VMEM((length, length), f32),
+    ]
+
+
+def run_forward(n_own, h_own, n_seq, heads_row, operands):
+    tokens, chan = operands[0].shape
+    length = tokens // n_own
+    pair_block = pl.BlockSpec((length, 128), lambda q, p: (q, p))
+    return pl.pallas_call(
+        functools.partial(scan_forward, h_own, n_seq, heads_row),
+        grid=(n_own, chan // 128),
+        in_specs=scan_specs(length, operands[2].shape[1]),
+        out_specs=[pair_block, pair_block],
+        out_shape=[
+            jax.ShapeDtypeStruct((tokens, chan), jnp.bfloat16),
+            jax.ShapeDtypeStruct((tokens, chan), jnp.float32),
+        ],
+        scratch_shapes=scan_scratch(length, h_own),
+        compiler_params=pltpu.CompilerParams(vmem_limit_bytes=48 << 20),
+        name="scan_forward",
+    )(*operands)
+
+
+def run_backward(n_own, h_own, n_seq, heads_row, operands, d_y, inner):
+    f32 = jnp.float32
+    tokens, chan = operands[0].shape
+    length = tokens // n_own
+    pair_block = pl.BlockSpec((length, 128), lambda q, p: (q, p))
+    return pl.pallas_call(
+        functools.partial(scan_backward, h_own, n_seq, heads_row),
+        grid=(n_own, chan // 128),
+        in_specs=scan_specs(length, operands[2].shape[1]) + [pair_block, pair_block],
+        out_specs=[
+            pair_block,
+            pl.BlockSpec((length, 2 * NST), lambda q, p: (q, 0)),
+            pl.BlockSpec((length, 128), lambda q, p: (q, 0)),
+            pl.BlockSpec((1, 8, 128), lambda q, p: (q, 0, p)),
+            pl.BlockSpec((1, 8, 2 * NST), lambda q, p: (q, 0, 0)),
+            pl.BlockSpec((1, 8, 128), lambda q, p: (q, 0, 0)),
+        ],
+        out_shape=[
+            jax.ShapeDtypeStruct((tokens, chan), jnp.bfloat16),
+            jax.ShapeDtypeStruct((tokens, 2 * NST), jnp.bfloat16),
+            jax.ShapeDtypeStruct((tokens, 128), f32),
+            jax.ShapeDtypeStruct((n_own, 8, chan), f32),
+            jax.ShapeDtypeStruct((n_own, 8, 2 * NST), f32),
+            jax.ShapeDtypeStruct((n_own, 8, 128), f32),
+        ],
+        scratch_shapes=scan_scratch(length, h_own)
+        + [
+            pltpu.VMEM((length, length), f32),
+            pltpu.VMEM((length, 128), f32),
+            pltpu.VMEM((length, 128), f32),
+        ],
+        compiler_params=pltpu.CompilerParams(vmem_limit_bytes=56 << 20),
+        name="scan_backward",
+    )(*operands, d_y, inner)
 
 
 def head_plan(
@@ -358,30 +663,22 @@
     x_raw = project[:, chan : 2 * chan].astype(bf16)
     bc_raw = project[:, 2 * chan : 2 * chan + 2 * NST].astype(bf16)
     dt_all = project[:, 2 * chan + 2 * NST :].astype(bf16)
-    dt_raw = own_head(dt_all.T).T
-    local_params = (
-        own_chan(conv_weight[:DI]),
-        own_chan(conv_bias[:DI]),
-        conv_weight[DI:],
-        conv_bias[DI:],
-        own_head(dt_bias),
-        own_head(a_log),
-        own_head(d_skip),
-    )
-
-    def head_mixer(x_values, step_raw, bc_values, params_in):
-        def single_seq(x_one, step_one, bc_one, seg_one):
-            return mixer(x_one, step_one, bc_one, seg_one, *params_in)
-
-        return jax.vmap(single_seq)(x_values, step_raw, bc_values, seg_all)
-
-    def by_seq(v):
-        return v.reshape(n_own, length, v.shape[-1]).astype(f32)
-
-    mixed, pull_mix = jax.vjp(
-        head_mixer, by_seq(x_raw), by_seq(dt_raw), by_seq(bc_raw), local_params
-    )
-    y = mixed.reshape(n_own * length, chan).astype(bf16).astype(f32)
+    wx = jnp.concatenate(
+        [
+            own_chan(conv_weight[:DI]).T,
+            own_chan(conv_bias[:DI])[None],
+            jnp.repeat(own_head(d_skip), HDIM)[None],
+            jnp.zeros((2, chan), f32),
+        ],
+        axis=0,
+    )
+    wbc = jnp.concatenate(
+        [conv_weight[DI:].T, conv_bias[DI:][None], jnp.zeros((3, 2 * NST), f32)], axis=0
+    )
+    head_vals = jnp.pad(jnp.stack([own_head(dt_bias), own_head(a_log)]), ((0, 6), (0, 128 - h_own)))
+    operands = (x_raw, bc_raw, dt_all, seg_all[:, :, None], seg_all[:, None, :], wx, wbc, head_vals)
+    y, inner = run_forward(n_own, h_own, n_seq, heads_row, operands)
+    y = y.astype(f32)
     gain = own_chan(gate_gain)
     sig = jax.nn.sigmoid(z)
     act = z * sig
@@ -406,16 +703,19 @@
     d_gate_gain = jnp.sum(d_gated * gr, axis=0)
     grad_out = jnp.einsum("tf,td->fd", gated, cot_all, preferred_element_type=f32)
     grad_out = lax.psum_scatter(grad_out, "dp", scatter_dimension=0, tiled=True)
-    d_x, d_dt, d_bc, d_params = pull_mix(by_seq(d_y))
+    d_x, d_bc, d_dt, g_x, g_bc, g_head = run_backward(
+        n_own, h_own, n_seq, heads_row, operands, d_y, inner
+    )
+    g_x, g_bc, g_head = jnp.sum(g_x, 0), jnp.sum(g_bc, 0), jnp.sum(g_head, 0)
     d_project = jnp.concatenate(
         [
-            d_z,
-            d_x.reshape(n_own * length, chan),
-            d_bc.reshape(n_own * length, 2 * NST),
-            spread_head(d_dt.reshape(n_own * length, h_own).T).T,
+            d_z.astype(bf16),
+            d_x,
+            d_bc,
+            spread_head(d_dt[:, :h_own].T).T.astype(bf16),
         ],
         axis=1,
-    ).astype(bf16)
+    )
     d_normed = lax.dot_general(
         d_project, w_in, (((1,), (1,)), ((), ())), preferred_element_type=f32
     ).astype(bf16)
@@ -435,14 +735,13 @@
         cotangent.astype(f32) + inv * dn - (inv * inv * inv) * along * hidden_f
     ).astype(bf16)
     d_norm_gain = jnp.sum(d_normed * hidden_f * inv, axis=(0, 1))
-    d_kernel_x, d_offset_x, d_kernel_bc, d_offset_bc, d_shift, d_decay, d_skip_part = d_params
     totals = lax.psum(
         (
-            jnp.concatenate([spread_chan(d_kernel_x), d_kernel_bc], axis=0),
-            jnp.concatenate([spread_chan(d_offset_x), d_offset_bc], axis=0),
-            spread_head(d_shift),
-            spread_head(d_decay),
-            spread_head(d_skip_part),
+            jnp.concatenate([spread_chan(g_x[:CONV].T), g_bc[:CONV].T], axis=0),
+            jnp.concatenate([spread_chan(g_x[CONV]), g_bc[CONV]], axis=0),
+            spread_head(g_head[0, :h_own]),
+            spread_head(g_head[1, :h_own]),
+            spread_head(jnp.sum(g_x[CONV + 1].reshape(h_own, HDIM), axis=1)),
             d_norm_gain,
             spread_chan(d_gate_gain),
         ),

time: 1010 us -> 881 us (0.87)
  matrix products: 141 us -> 55.5 us
  local copies, waits for them, and re-layouts: 94.7 us -> 24.5 us
  other arithmetic: 74.8 us -> 16.2 us
  waiting for transfers between devices: 511 us -> 562 us
  Pallas kernels: 0 us -> 40 us
    dot_general x28 -> x0, matrix products: 81.8 us -> none  [the longest x6 41.5 us: advance(): jnp.einsum('hij,jhp->ihp', scores, block_vals, precision=lax.Precision.HI...]
    all_gather x1, waiting for transfers between devices: 25.3 us -> 73.6 us  [head_plan(): lax.all_gather(cotangent, 'seq', axis=1, tiled=True)]
    pallas_call x0 -> x2, Pallas kernels: none -> 40 us  [the longest x1 27.2 us: run_backward(): pl.pallas_call(functools.partial(scan_backward, h_own, n_seq, heads_row),...]
    another operation x19 -> x1, other arithmetic: 27.9 us -> 0.01 us  [head_plan(): jnp.stack([own_head(dt_bias), own_head(a_log)])]
    transpose x5, local copies, waits for them, and re-layouts: 15.2 us -> 1.18 us  [the longest x2 1.18 us: head_plan(): d_dt[:, :h_own]]
    reshape x9 -> x1, local copies, waits for them, and re-layouts: 13.6 us -> 0.09 us  [own_head(): return lax.dynamic_index_in_dim(vec.reshape((n_dp, n_seq, heads_row) + ve...]
    squeeze x14 -> x0, local copies, waits for them, and re-layouts: 10.3 us -> none  [the longest x12 10.3 us: state_scan(): unused, outputs = lax.scan(jax.checkpoint(advance), initial, pieces)]
    another operation x28 -> x12, local copies, waits for them, and re-layouts: 10.7 us -> 0.51 us  [the longest x2 0.17 us: spread_head(): piece = vec.reshape((n_dp, 1, heads_row) + vec.shape[1:])]
  transfers between devices with their start and end apart: 12 -> 12, of which waited for: 8 -> 9; matrix products, arithmetic and copies ran while one was open for 12% -> 7% of each run, Pallas kernels for 0% -> 1%
where the time goes in v2:
time: 881 us; the launch traced here: 873 us
  waiting for transfers between devices  562 us (64%)
  blocking collectives  147 us (17%)
  matrix products  55.5 us (6%)
  Pallas kernels  40 us (5%)
  local copies, waits for them, and re-layouts  24.5 us (3%)
  other arithmetic  16.2 us (2%)
  between operations  15.3 us (2%)
  starting transfers between devices  13.6 us (2%)
    psum x1, waiting for transfers between devices, head_plan(): lax.psum((jnp.concatenate([spread_chan(g_x[:CONV].T), g_bc[:CONV].T], axi...  122 us
    reduce_scatter x1, waiting for transfers between devices, head_plan(): lax.psum_scatter(d_normed.reshape(n_own, length, width), 'seq', scatter_d...  96.5 us
    all_gather x1, waiting for transfers between devices, head_plan(): lax.all_gather(cotangent, 'seq', axis=1, tiled=True)  73.6 us
    reduce_scatter x1, waiting for transfers between devices, head_plan(): grad_in = lax.psum_scatter(grad_in, 'dp', scatter_dimension=0, tiled=True)  66.5 us
    all_gather x1, blocking collectives, head_plan(): tail = lax.all_gather(in_weight[:, 2 * DI:], 'seq', axis=0, tiled=True)  64.1 us
    reduce_scatter x1, waiting for transfers between devices, head_plan(): lax.psum_scatter(grad_in[:, 2 * chan:], 'seq', scatter_dimension=0, tiled...  58.6 us
    reduce_scatter x1, waiting for transfers between devices, head_plan(): grad_out = lax.psum_scatter(grad_out, 'dp', scatter_dimension=0, tiled=True)  49.9 us
    reduce_scatter x1, waiting for transfers between devices, head_plan(): lax.psum_scatter(part.reshape(n_own, length, width), 'seq', scatter_dimen...  47.8 us
  transfers between devices with their start and end apart: 12, of which 9 were waited for; matrix products, arithmetic and copies ran while one was open for 7% of the time, Pallas kernels for 1%

profile of v2, /device:TPU:0, one launch (start us, length us, event | category | flops | bytes accessed | tf_op | source)
XLA Modules:
  0.0 873.0 jit_solution(6210377890232359002)
XLA Ops:
  12.4 7.3 all-to-all-start
  19.7 64.1 %all_gather.19 = bf16[512,320]{1,0:T(8,128)(2,1)S(1)} all-gather(bf16[64,320]{1,0:T(8,128)(2,1)S(1)} %slice-done.1), channel_id=1, replica_groups=mesh['dp'=4,'seq'=8] {'seq'}, dimensions={0}, use_global_device_ids=true | all-gather | bytes 368640 | tf_op jit(solution)/shard_map/all_gather | solution.py:629
  88.1 19.5 %all-gather = s32[8,64,2]{1,2,0:T(2,128)S(1)} all-gather(s32[1,64,2]{1,2,0:T(2,128)S(1)} %bitcast.134), channel_id=1, replica_groups=mesh['dp'=4,'seq'=8] {'seq'}, dimensions={0}, use_global_device_ids=true | all-gather | bytes 4608 | tf_op jit(solution)/shard_map/all_gather | solution.py:633
  109.7 44.4 %all-gather.8.cloned.1.call-done = bf16[2048,1344]{1,0:T(8,128)(2,1)} async-done(((bf16[512,1344]{1,0:T(8,128)(2,1)}), bf16[2048,1344]{1,0:T(8,128)(2,1)}) %all-gather.8.cloned.1.call-update) | async-done | bytes 5505040 | tf_op jit(solution)/shard_map/all_gather | solution.py:630
  154.1 11.7 %fusion.22 = (bf16[1024,1344]{1,0:T(8,128)(2,1)S(1)}, f32[1024,1344]{1,0:T(8,128)}) fusion(bf16[1024,2048]{1,0:T(8,128)(2,1)} %bitcast.137, bf16[2048,1344]{1,0:T(8,128)(2,1)} %all-gather.8.cloned.1.call-done), kind=kOutput, calls=%fused_computation.77 | convolution fusion | flops 5638520832 | bytes 17956864 | tf_op jit(solution)/shard_map/dot_general | solution.py:661
  166.0 12.8 %scan_forward.1 = (bf16[1024,512]{1,0:T(8,128)(2,1)S(1)}, f32[1024,512]{1,0:T(8,128)S(1)}) custom-call(bf16[1024,512]{1,0:T(8,128)(2,1)S(1)} %slice.91.x_ref, bf16[1024,256]{1,0:T(8,128)(2,1)S(1)} %slice.92.bc_ref, bf16[1024,64]{1,0:T(8,128)(2,1)S(1)} %slice.93.dt_ref, s32[2,512,1]{2,1,0:T(8,128)S(1)} %copy.78.segc_ref, ...), custom_call_target="tpu_custom_call" | custom-call | tf_op jit(solution)/shard_map/scan_forward/pallas_call | solution.py:548
  180.1 73.6 %all-gather.10.cloned.1.call-done = bf16[2,512,2048]{2,1,0:T(8,128)(2,1)} async-done(((bf16[2,64,2048]{2,1,0:T(8,128)(2,1)}), bf16[2,512,2048]{2,1,0:T(8,128)(2,1)}) %all-gather.10.cloned.1.call-update) | async-done | bytes 4194320 | tf_op jit(solution)/shard_map/all_gather | solution.py:632
  253.7 7.6 multiply_reduce_fusion.2
  261.3 19.1 %psum.56 = f32[2,1024]{1,0:T(2,128)S(1)} all-reduce(f32[2,1024]{1,0:T(2,128)S(1)} %pad_maximum_fusion.7), channel_id=1, replica_groups=mesh['dp'=4,'seq'=8] {'seq'}, use_global_device_ids=true, to_apply=%region_3.4 | all-reduce | flops 2048 | bytes 16384 | tf_op jit(solution)/shard_map/psum | solution.py:690
  280.5 4.2 fusion.1
  284.7 27.2 %scan_backward.1 = (bf16[1024,512]{1,0:T(8,128)(2,1)}, bf16[1024,256]{1,0:T(8,128)(2,1)}, f32[1024,128]{1,0:T(8,128)}, f32[2,8,512]{2,1,0:T(8,128)}, f32[2,8,256]{2,1,0:T(8,128)}, /*index=5*/f32[2,8,128]{2,1,0:T(8,128)}) custom-call(bf16[1024,512]{1,0:T(8,128)(2,1)} %copy-done.2, bf16[1024,256]{1,0:T(8,128)(2,1)} %copy-done.4, bf16[1024,64]{1,0:T(8,128)(2,1)} %copy-done.5, ...), custom_call_target="tpu_custom_call" | custom-call | tf_op jit(solution)/shard_map/scan_backward/pallas_call | solution.py:568
  313.4 10.5 %fusion.14 = f32[2048,1344]{0,1:T(8,128)} fusion(bf16[1024,2048]{1,0:T(8,128)(2,1)} %bitcast.138, bf16[1024,64]{1,0:T(8,128)(2,1)S(1)} %bitcast.105, bf16[1024,256]{1,0:T(8,128)(2,1)} %get-tuple-element.22, bf16[1024,512]{1,0:T(8,128)(2,1)} %get-tuple-element.21, bf16[1024,512]{1,0:T(8,128)(2,1)S(1)} %get-tuple-element.39), kind=kOutput, calls=%fused_computation.37 | convolution fusion | flops 5648154624 | bytes 17956864 | tf_op jit(solution)/shard_map/td,tf->df/dot_general | solution.py:725
  325.0 10.8 %convolution_convert_fusion = bf16[1024,2048]{1,0:T(8,128)(2,1)} fusion(bf16[2048,1344]{1,0:T(8,128)(2,1)} %all-gather.8.cloned.1.call-done, bf16[1024,64]{1,0:T(8,128)(2,1)S(1)} %bitcast.106, bf16[1024,256]{1,0:T(8,128)(2,1)S(1)} %copy-done.24, bf16[1024,512]{1,0:T(8,128)(2,1)} %get-tuple-element.21, bf16[1024,512]{1,0:T(8,128)(2,1)S(1)} %get-tuple-element.39), kind=kOutput, calls=%fused_computation | convolution fusion | flops 5650251776 | bytes 12451840 | tf_op jit(solution)/shard_map/dot_general | solution.py:719
  335.9 7.6 convolution_convert_fusion.1
  343.6 66.5 %reduce-scatter.12.cloned.1.call-done = f32[512,1344]{0,1:T(8,128)} async-done(((f32[2048,1344]{0,1:T(8,128)}), f32[512,1344]{0,1:T(8,128)}) %reduce-scatter.12.cloned.1.call-update) | async-done | bytes 2752528 | tf_op jit(solution)/shard_map/reduce_scatter | solution.py:726
  413.4 7.3 fusion.21
  424.7 3.8 copy.86
  428.6 5.7 all-to-all-start.1
  435.3 96.5 %reduce-scatter.10.cloned.1.call-done = bf16[2,64,2048]{2,1,0:T(8,128)(2,1)} async-done(((bf16[2,512,2048]{2,1,0:T(8,128)(2,1)}), bf16[2,64,2048]{2,1,0:T(8,128)(2,1)}) %reduce-scatter.10.cloned.1.call-update) | async-done | bytes 524304 | tf_op jit(solution)/shard_map/reduce_scatter | solution.py:722
  533.2 43.8 %all-reduce.1 = (f32[4352]{0:T(1024)}, f32[64]{0:T(128)}, f32[64]{0:T(128)}, f32[64]{0:T(128)}, f32[2048]{0:T(1024)}, /*index=5*/f32[4096]{0:T(1024)}) all-reduce(f32[4352]{0:T(1024)S(1)} %pad_maximum_fusion.6, f32[64]{0:T(128)S(1)} %reshape.180, f32[64]{0:T(128)S(1)} %reshape.181, ...), channel_id=1, replica_groups=mesh['dp'=4,'seq'=8] {'dp','seq'}, use_global_device_ids=true, to_apply=%region_12.13 | all-reduce | flops 10688 | bytes 85504 | tf_op jit(solution)/shard_map/psum | solution.py:738
  577.0 47.8 %reduce-scatter.8.cloned.1.call-done = bf16[2,64,2048]{2,1,0:T(8,128)(2,1)} async-done(((bf16[2,512,2048]{2,1,0:T(8,128)(2,1)}), bf16[2,64,2048]{2,1,0:T(8,128)(2,1)}) %reduce-scatter.8.cloned.1.call-update) | async-done | bytes 524304 | tf_op jit(solution)/shard_map/reduce_scatter | solution.py:696
  631.8 58.6 %reduce-scatter.16.cloned.1.call-done = f32[64,320]{1,0:T(8,128)} async-done(((f32[512,320]{1,0:T(8,128)}), f32[64,320]{1,0:T(8,128)}) %reduce-scatter.16.cloned.1.call-update) | async-done | bytes 81936 | tf_op jit(solution)/shard_map/reduce_scatter | solution.py:730
  692.8 121.5 %all-reduce.4.cloned.1.call-done = f32[4352,4]{0,1:T(4,128)} async-done(((f32[4352,4]{0,1:T(4,128)}), f32[4352,4]{0,1:T(4,128)}) %all-reduce.4.cloned.1.call-update) | async-done | bytes 69648 | tf_op jit(solution)/shard_map/psum | solution.py:738
  814.3 49.9 %reduce-scatter.14.cloned.1.call-done = f32[128,2048]{1,0:T(8,128)} async-done(((f32[512,2048]{1,0:T(8,128)}), f32[128,2048]{1,0:T(8,128)}) %reduce-scatter.14.cloned.1.call-update) | async-done | bytes 1048592 | tf_op jit(solution)/shard_map/reduce_scatter | solution.py:705
  (172 shorter events, 35.9 us)
Async XLA Ops:
  7.2 100.9 %copy-start = (f32[4096]{0:T(1024)S(1)}, f32[4096]{0:T(1024)}, u32[]{:S(2)}) copy-start(f32[4096]{0:T(1024)} %param.21) | copy-start | bytes 49156
  7.2 102.5 %all-gather.6.cloned.1.call-start = ((), (), s32[]{:S(2)}) async-start(), calls=%async_computation.7 | async-start | bytes 4718592 | tf_op jit(solution)/shard_map/all_gather | solution.py:625
  12.4 71.4 %all-to-all-start = ((bf16[64,2,4,8,128]{4,2,1,0,3:T(4,128)(2,1)}), bf16[64,2,4,8,128]{4,2,1,0,3:T(4,128)(2,1)S(1)}, u32[]{:S(2)}, u32[]{:S(2)}) async-start(bf16[64,2,4,8,128]{4,2,1,0,3:T(4,128)(2,1)} %copy.74), calls=%async_computation | async-start | bytes 2097152 | tf_op jit(solution)/shard_map/all_to_all | solution.py:627
  19.6 134.4 %all-gather.8.cloned.1.call-start = ((), (), s32[]{:S(2)}) async-start(), calls=%async_computation.8 | async-start | bytes 7208960 | tf_op jit(solution)/shard_map/all_gather | solution.py:630
  85.8 94.3 %all-gather.12.cloned.1.call-start = ((), (), s32[]{:S(2)}) async-start(), calls=%async_computation.10 | async-start | bytes 2621440 | tf_op jit(solution)/shard_map/all_gather | solution.py:631
  86.6 167.1 %all-gather.10.cloned.1.call-start = ((), (), s32[]{:S(2)}) async-start(), calls=%async_computation.9 | async-start | bytes 4718592 | tf_op jit(solution)/shard_map/all_gather | solution.py:632
  87.2 322.9 %reduce-scatter.12.cloned.1.call-start = ((), (), s32[]{:S(2)}) async-start(), calls=%async_computation.13 | async-start | bytes 13762560 | tf_op jit(solution)/shard_map/reduce_scatter | solution.py:726
  107.9 58.0 %copy-start.3 = (s32[2,512,1]{2,1,0:T(8,128)}, s32[2,512,1]{2,1,0:T(8,128)S(1)}, u32[]{:S(2)}) copy-start(s32[2,512,1]{2,1,0:T(8,128)S(1)} %copy.78.segc_ref) | copy-start | bytes 12292
  107.9 58.0 %copy-start.10 = (s32[2,1,512]{2,1,0:T(1,128)}, s32[2,1,512]{2,1,0:T(1,128)S(1)}, u32[]{:S(2)}) copy-start(s32[2,1,512]{2,1,0:T(1,128)S(1)} %broadcast_in_dim.31.segr_ref) | copy-start | bytes 12292
  165.8 95.5 %copy-start.2 = (bf16[1024,512]{1,0:T(8,128)(2,1)}, bf16[1024,512]{1,0:T(8,128)(2,1)S(1)}, u32[]{:S(2)}) copy-start(bf16[1024,512]{1,0:T(8,128)(2,1)S(1)} %slice.91.x_ref) | copy-start | bytes 3145732
  165.9 95.4 %copy-start.4 = (bf16[1024,256]{1,0:T(8,128)(2,1)}, bf16[1024,256]{1,0:T(8,128)(2,1)S(1)}, u32[]{:S(2)}) copy-start(bf16[1024,256]{1,0:T(8,128)(2,1)S(1)} %slice.92.bc_ref) | copy-start | bytes 1572868
  166.0 95.3 %copy-start.5 = (bf16[1024,64]{1,0:T(8,128)(2,1)}, bf16[1024,64]{1,0:T(8,128)(2,1)S(1)}, u32[]{:S(2)}) copy-start(bf16[1024,64]{1,0:T(8,128)(2,1)S(1)} %slice.93.dt_ref) | copy-start | bytes 393220
  324.0 207.9 %reduce-scatter.10.cloned.1.call-start = ((), (), s32[]{:S(2)}) async-start(), calls=%async_computation.12 | async-start | bytes 4718592 | tf_op jit(solution)/shard_map/reduce_scatter | solution.py:722
  335.8 289.0 %reduce-scatter.8.cloned.1.call-start = ((), (), s32[]{:S(2)}) async-start(), calls=%async_computation.11 | async-start | bytes 4718592 | tf_op jit(solution)/shard_map/reduce_scatter | solution.py:696
  343.5 68.9 %copy-start.16 = (f32[2,8,512]{2,1,0:T(8,128)S(1)}, f32[2,8,512]{2,1,0:T(8,128)}, u32[]{:S(2)}) copy-start(f32[2,8,512]{2,1,0:T(8,128)} %get-tuple-element.24) | copy-start | bytes 98308
  343.5 69.1 %copy-start.17 = (f32[2,8,256]{2,1,0:T(8,128)S(1)}, f32[2,8,256]{2,1,0:T(8,128)}, u32[]{:S(2)}) copy-start(f32[2,8,256]{2,1,0:T(8,128)} %get-tuple-element.25) | copy-start | bytes 49156
  343.5 346.9 %reduce-scatter.16.cloned.1.call-start = ((), (), s32[]{:S(2)}) async-start(), calls=%async_computation.16 | async-start | bytes 884736 | tf_op jit(solution)/shard_map/reduce_scatter | solution.py:730
  412.4 401.9 %all-reduce.4.cloned.1.call-start = ((), (), s32[]{:S(2)}) async-start(), calls=%async_computation.14 | async-start | bytes 139264 | tf_op jit(solution)/shard_map/psum | solution.py:738
  413.3 450.9 %reduce-scatter.14.cloned.1.call-start = ((), (), s32[]{:S(2)}) async-start(), calls=%async_computation.15 | async-start | bytes 5242880 | tf_op jit(solution)/shard_map/reduce_scatter | solution.py:705
  428.5 103.3 %copy-start.11 = (bf16[2,64,2048]{2,1,0:T(8,128)(2,1)S(1)}, bf16[2,64,2048]{2,1,0:T(8,128)(2,1)}, u32[]{:S(2)}) copy-start(bf16[2,64,2048]{2,1,0:T(8,128)(2,1)} %param.12) | copy-start | bytes 1572868
  428.5 103.3 %copy-start.14 = (f32[2048]{0:T(1024)S(1)}, f32[2048]{0:T(1024)}, u32[]{:S(2)}) copy-start(f32[2048]{0:T(1024)} %param.20) | copy-start | bytes 24580
  428.5 196.3 %copy-start.12 = (bf16[2,64,2048]{2,1,0:T(8,128)(2,1)S(1)}, bf16[2,64,2048]{2,1,0:T(8,128)(2,1)}, u32[]{:S(2)}) copy-start(bf16[2,64,2048]{2,1,0:T(8,128)(2,1)} %param.23) | copy-start | bytes 1572868
  428.6 198.9 %all-to-all-start.1 = ((f32[8,64,2,4,1,128]{5,3,2,1,4,0:T(4,128)}), f32[8,64,2,4,1,128]{5,3,2,1,4,0:T(4,128)S(1)}, u32[]{:S(2)}, u32[]{:S(2)}) async-start(f32[8,64,2,4,1,128]{5,3,2,1,4,0:T(4,128)} %copy.86), calls=%async_computation.4 | async-start | bytes 4194304 | tf_op jit(solution)/shard_map/all_to_all | solution.py:728
  630.0 235.7 %copy-start.1 = (f32[4096]{0:T(1024)S(1)}, f32[4096]{0:T(1024)}, u32[]{:S(2)}) copy-start(f32[4096]{0:T(1024)} %param.21) | copy-start | bytes 49156
  (16 other events, 250.3 us)
Sparse Core Ops, SparseCore 0:
  10.8 98.8 all-gather.5
  111.8 42.1 all-gather.7
  155.6 22.5 all-gather.11
  180.3 73.3 all-gather.9
  324.1 85.9 reduce-scatter.11
  413.6 118.1 reduce-scatter.9
  535.9 88.9 reduce-scatter.7
  628.1 62.2 reduce-scatter.15
  697.5 116.8 all-reduce.3
  817.4 46.7 reduce-scatter.13

commit v3 on v2

--- a/solution.py
+++ b/solution.py
@@ -596,6 +596,276 @@
     )(*operands, d_y, inner)
 
 
+MESH = pl.DeviceIdType.MESH
+WIDE = 8
+
+
+def place():
+    dp, s = lax.axis_index("dp"), lax.axis_index("seq")
+    z, x = s // 2, s % 2
+    y, core = dp // 2, dp % 2
+    return dp, s, z, x, s + 1 - 2 * x, dp + 2 - 4 * y, dp + 1 - 2 * core
+
+
+def greet(peers):
+    barrier = pltpu.get_barrier_semaphore()
+    for device in peers:
+        pl.semaphore_signal(barrier, inc=1, device_id=device, device_id_type=MESH)
+    pl.semaphore_wait(barrier, len(peers))
+
+
+def remote(src, dst, send, recv, device):
+    return pltpu.make_async_remote_copy(
+        src_ref=src, dst_ref=dst, send_sem=send, recv_sem=recv, device_id=device, device_id_type=MESH
+    )
+
+
+class TokenGather:
+    def __init__(self, own, full, send, recv, where):
+        self.own, self.full, self.send, self.recv = own, full, send, recv
+        self.dp, self.s, self.z, self.x, self.x_peer, _, _ = where
+        self.span = own.shape[1]
+
+    def part(self, shard, q):
+        return self.full.at[q, pl.ds(pl.multiple_of(shard * self.span, self.span), self.span)]
+
+    def copy(self, shard_z, way, q, mine):
+        shard = shard_z * 2 + self.x
+        target = (self.s + 2, self.s - 2, self.x_peer)[way]
+        src = self.own.at[q] if mine else self.part(shard, q)
+        return remote(
+            src, self.part(shard, q), self.send.at[way, shard_z, q], self.recv.at[shard, q], (self.dp, target)
+        )
+
+    def arrived(self, shard, q):
+        part = self.part(shard, q)
+        remote(part, part, self.send.at[0, 0, q], self.recv.at[shard, q], (self.dp, self.x_peer)).wait_recv()
+
+    def start(self, q):
+        @pl.when(self.z < 3)
+        def up():
+            self.copy(self.z, 0, q, True).start()
+
+        @pl.when(self.z > 0)
+        def down():
+            self.copy(self.z, 1, q, True).start()
+
+        self.copy(self.z, 2, q, True).start()
+
+    def step(self, hop, q):
+        @pl.when(self.z >= hop)
+        def from_below():
+            shard_z = self.z - hop
+            self.arrived(shard_z * 2 + self.x, q)
+
+            @pl.when(self.z < 3)
+            def up():
+                self.copy(shard_z, 0, q, False).start()
+
+            self.copy(shard_z, 2, q, False).start()
+
+        @pl.when(self.z + hop <= 3)
+        def from_above():
+            shard_z = self.z + hop
+            self.arrived(shard_z * 2 + self.x, q)
+
+            @pl.when(self.z > 0)
+            def down():
+                self.copy(shard_z, 1, q, False).start()
+
+            self.copy(shard_z, 2, q, False).start()
+
+    def finish(self, q):
+        for shard_z in range(4):
+            self.arrived(shard_z * 2 + 1 - self.x, q)
+        for shard_z in range(4):
+            self.copy(shard_z, 2, q, False).wait_send()
+
+            @pl.when((self.z < 3) & (self.z >= shard_z))
+            def up():
+                self.copy(shard_z, 0, q, False).wait_send()
+
+            @pl.when((self.z > 0) & (self.z <= shard_z))
+            def down():
+                self.copy(shard_z, 1, q, False).wait_send()
+
+
+def gather_kernel(normed, cot, in_w, out_w, seg, n_all, c_all, w_in, w_out, seg_all,
+                  n_send, n_recv, c_send, c_recv, wide_send, tail_send, wide_recv, tail_recv,
+                  y_send, core_send, cross_send, block_recv, out_send, out_recv, seg_send, seg_recv, local):
+    where = place()
+    dp, s, z, x, x_peer, y_peer, core_peer = where
+    peers = [(dp, (s + k) % 8) for k in range(1, 8)] + [(y_peer, s), (core_peer, s)]
+    greet(peers)
+    in_rows, rows = in_w.shape[0], out_w.shape[0]
+    chan = w_out.shape[0]
+    tail = in_w.shape[1] - 2 * DI
+
+    def block(d, shard, lo=0, size=None):
+        size = w_in.shape[1] if size is None else size
+        at = pl.multiple_of((d * 8 + shard) * in_rows, in_rows)
+        return w_in.at[pl.ds(at, in_rows), pl.ds(lo, size)]
+
+    def wide_src(piece, target):
+        at = pl.multiple_of((piece * 8 + target) * rows, rows)
+        return in_w.at[:, pl.ds(at, rows)]
+
+    tail_src = in_w.at[:, pl.ds(2 * DI, tail)]
+
+    def push(k, _):
+        target = (s + k) % 8
+        remote(seg, seg_all.at[s], seg_send.at[k], seg_recv.at[s], (dp, target)).start()
+        for piece in range(WIDE):
+            remote(
+                wide_src(piece, target), block(dp, s, piece * rows, rows), wide_send.at[k], wide_recv.at[s],
+                (dp, target),
+            ).start()
+        remote(tail_src, block(dp, s, 2 * chan, tail), tail_send.at[k], tail_recv.at[s], (dp, target)).start()
+        return 0
+
+    lax.fori_loop(1, 8, push, 0)
+    tokens = TokenGather(normed, n_all, n_send, n_recv, where)
+    cots = TokenGather(cot, c_all, c_send, c_recv, where)
+    for q in range(2):
+        tokens.start(q)
+    own_copies = []
+    for piece in range(WIDE):
+        own_copies.append(pltpu.make_async_copy(wide_src(piece, s), block(dp, s, piece * rows, rows), local.at[piece]))
+    own_copies.append(pltpu.make_async_copy(tail_src, block(dp, s, 2 * chan, tail), local.at[8]))
+    later_copies = [
+        pltpu.make_async_copy(out_w, w_out.at[pl.ds(pl.multiple_of(dp * rows, rows), rows)], local.at[9]),
+        pltpu.make_async_copy(seg, seg_all.at[s], local.at[10]),
+    ]
+    for q in range(2):
+        later_copies.append(pltpu.make_async_copy(normed.at[q], tokens.part(s, q), local.at[11 + q]))
+        later_copies.append(pltpu.make_async_copy(cot.at[q], cots.part(s, q), local.at[13 + q]))
+    for copy in own_copies + later_copies:
+        copy.start()
+    for copy in own_copies:
+        copy.wait()
+
+    def spread(shard, shard_sem):
+        remote(block(dp, shard), block(dp, shard), y_send.at[shard_sem], block_recv.at[dp, shard], (y_peer, s)).start()
+        remote(
+            block(dp, shard), block(dp, shard), core_send.at[shard_sem], block_recv.at[dp, shard], (core_peer, s)
+        ).start()
+
+    spread(s, 0)
+    out_block = w_out.at[pl.ds(pl.multiple_of(dp * rows, rows), rows)]
+
+    def forward(k, _):
+        source = (s + 8 - k) % 8
+        remote(
+            block(dp, source, 0, 2 * chan), block(dp, source, 0, 2 * chan), wide_send.at[k], wide_recv.at[source],
+            (dp, x_peer),
+        ).wait_recv()
+        remote(
+            block(dp, source, 2 * chan, tail), block(dp, source, 2 * chan, tail), tail_send.at[k],
+            tail_recv.at[source], (dp, x_peer),
+        ).wait_recv()
+        spread(source, k)
+        return 0
+
+    def cross(k, _):
+        source = (s + 8 - k) % 8
+        there = block(y_peer, source)
+        copy = remote(there, there, cross_send.at[k], block_recv.at[y_peer, source], (core_peer, s))
+        copy.wait_recv()
+        copy.start()
+        return 0
+
+    tokens.step(1, 0)
+    lax.fori_loop(1, 4, forward, 0)
+    tokens.step(1, 1)
+    lax.fori_loop(4, 8, forward, 0)
+    tokens.step(2, 0)
+    lax.fori_loop(0, 4, cross, 0)
+    tokens.step(2, 1)
+    lax.fori_loop(4, 8, cross, 0)
+    tokens.step(3, 0)
+    tokens.step(3, 1)
+    for q in range(2):
+        cots.start(q)
+
+    def out_part(d):
+        return w_out.at[pl.ds(pl.multiple_of(d * rows, rows), rows)]
+
+    remote(out_w, out_part(dp), out_send.at[0], out_recv.at[dp], (y_peer, s)).start()
+    remote(out_w, out_part(dp), out_send.at[1], out_recv.at[dp], (core_peer, s)).start()
+    for hop in range(1, 4):
+        for q in range(2):
+            cots.step(hop, q)
+    out_cross = remote(out_part(y_peer), out_part(y_peer), out_send.at[2], out_recv.at[y_peer], (core_peer, s))
+    out_cross.wait_recv()
+    out_cross.start()
+    for q in range(2):
+        tokens.finish(q)
+        cots.finish(q)
+    for copy in later_copies:
+        copy.wait()
+
+    def settle(k, _):
+        shard = (s + 8 - k) % 8
+        for d in (core_peer, core_peer + y_peer - dp):
+            there = block(d, shard)
+            remote(there, there, core_send.at[k], block_recv.at[d, shard], (core_peer, s)).wait_recv()
+        there = block(dp, shard)
+        remote(there, there, y_send.at[k], block_recv.at[dp, shard], (y_peer, s)).wait_send()
+        remote(there, there, core_send.at[k], block_recv.at[dp, shard], (core_peer, s)).wait_send()
+        remote(there, there, cross_send.at[k], block_recv.at[dp, shard], (core_peer, s)).wait_send()
+        return 0
+
+    lax.fori_loop(0, 8, settle, 0)
+
+    def settle_push(k, _):
+        source = (s + 8 - k) % 8
+        remote(seg, seg_all.at[source], seg_send.at[k], seg_recv.at[source], (dp, x_peer)).wait_recv()
+        remote(seg, seg_all.at[source], seg_send.at[k], seg_recv.at[source], (dp, x_peer)).wait_send()
+        remote(
+            block(dp, source, 0, 2 * chan), block(dp, source, 0, 2 * chan), wide_send.at[k], wide_recv.at[source],
+            (dp, x_peer),
+        ).wait_send()
+        remote(
+            block(dp, source, 2 * chan, tail), block(dp, source, 2 * chan, tail), tail_send.at[k],
+            tail_recv.at[source], (dp, x_peer),
+        ).wait_send()
+        return 0
+
+    lax.fori_loop(1, 8, settle_push, 0)
+    for d in (core_peer, core_peer + y_peer - dp):
+        remote(out_part(d), out_part(d), out_send.at[0], out_recv.at[d], (core_peer, s)).wait_recv()
+    for k in range(3):
+        remote(out_w, out_part(dp), out_send.at[k], out_recv.at[dp], (core_peer, s)).wait_send()
+
+
+def run_gather(normed, cot, in_w, out_w, seg):
+    bf16 = jnp.bfloat16
+    n_own, span, width = normed.shape
+    in_rows, rows = in_w.shape[0], out_w.shape[0]
+    chan = 4 * rows
+    columns = 2 * chan + in_w.shape[1] - 2 * DI
+    sem = pltpu.SemaphoreType.DMA
+    return pl.pallas_call(
+        gather_kernel,
+        in_specs=[pl.BlockSpec(memory_space=pl.ANY)] * 5,
+        out_specs=[pl.BlockSpec(memory_space=pl.ANY)] * 5,
+        out_shape=[
+            jax.ShapeDtypeStruct((n_own, 8 * span, width), bf16),
+            jax.ShapeDtypeStruct((n_own, 8 * span, width), bf16),
+            jax.ShapeDtypeStruct((32 * in_rows, columns), bf16),
+            jax.ShapeDtypeStruct((chan, width), bf16),
+            jax.ShapeDtypeStruct((8, 8, 128), jnp.float32),
+        ],
+        scratch_shapes=[
+            sem((3, 4, 2)), sem((8, 2)), sem((3, 4, 2)), sem((8, 2)),
+            sem((8,)), sem((8,)), sem((8,)), sem((8,)),
+            sem((8,)), sem((8,)), sem((8,)), sem((4, 8)), sem((3,)), sem((4,)), sem((8,)), sem((8,)), sem((15,)),
+        ],
+        compiler_params=pltpu.CompilerParams(collective_id=0, has_side_effects=True),
+        name="gather",
+    )(normed, cot, in_w, out_w, seg)
+
+
 def head_plan(
     hidden,
     segments,
@@ -622,15 +892,13 @@
     hidden_f = hidden.astype(f32)
     inv = lax.rsqrt(jnp.mean(hidden_f * hidden_f, axis=-1, keepdims=True) + 1e-05)
     normed = (hidden_f * inv * norm_gain).astype(bf16)
-    normed_all = lax.all_gather(normed, "seq", axis=1, tiled=True).reshape(n_own * length, width)
-    wide = in_weight[:, : 2 * DI].reshape(in_rows, 2, n_dp, n_seq, rows)
-    wide = lax.all_to_all(wide, "seq", split_axis=3, concat_axis=0, tiled=True)
-    wide = wide.reshape(n_seq * in_rows, 2 * chan)
-    tail = lax.all_gather(in_weight[:, 2 * DI :], "seq", axis=0, tiled=True)
-    w_in = lax.all_gather(jnp.concatenate([wide, tail], axis=1), "dp", axis=0, tiled=True)
-    w_out = lax.all_gather(out_weight, "dp", axis=0, tiled=True)
-    cot_all = lax.all_gather(cotangent, "seq", axis=1, tiled=True).reshape(n_own * length, width)
-    seg_all = lax.all_gather(segments, "seq", axis=1, tiled=True)
+    seg_tile = jnp.pad(segments.astype(f32), ((0, 8 - n_own), (0, 128 - shard_len)))
+    normed_all, cot_all, w_in, w_out, seg_all = run_gather(
+        normed, cotangent, in_weight, out_weight, seg_tile
+    )
+    normed_all = normed_all.reshape(n_own * length, width)
+    cot_all = cot_all.reshape(n_own * length, width)
+    seg_all = seg_all[:, :n_own, :shard_len].swapaxes(0, 1).reshape(n_own, length)
 
     def own_chan(vec):
         return lax.dynamic_index_in_dim(
@@ -751,7 +1019,7 @@
 
 
 def solution(mesh):
-    whole_heads = (DI // mesh.size) % HDIM == 0
+    whole_heads = mesh.shape["dp"] == 4 and mesh.shape["seq"] == 8
     shards = head_plan if whole_heads else general_plan
     placed = (
         P("dp", "seq", None),

time: 881 us -> 668 us (0.76)
  waiting for transfers between devices: 562 us -> 314 us
  Pallas kernels: 40 us -> 166 us
  blocking collectives: 147 us -> 63 us
    pallas_call x0 -> x1, Pallas kernels: none -> 126 us  [run_gather(): pl.pallas_call(gather_kernel, in_specs=[pl.BlockSpec(memory_space=pl.ANY)...]
    psum x1, waiting for transfers between devices: 122 us -> 0.01 us  [head_plan(): lax.psum((jnp.concatenate([spread_chan(g_x[:CONV].T), g_bc[:CONV].T], axi...]
    all_gather x4 -> x0, waiting for transfers between devices: 119 us -> none  [the longest x1 73.6 us: head_plan(): lax.all_gather(cotangent, 'seq', axis=1, tiled=True)]
    all_gather x2 -> x0, blocking collectives: 83.6 us -> none  [the longest x1 64.1 us: head_plan(): tail = lax.all_gather(in_weight[:, 2 * DI:], 'seq', axis=0, tiled=True)]
  transfers between devices with their start and end apart: 12 -> 7, of which waited for: 9 -> 5; matrix products, arithmetic and copies ran while one was open for 7% -> 7% of each run, Pallas kernels for 1% -> 0%
where the time goes in v3:
time: 668 us; the launch traced here: 660 us
  waiting for transfers between devices  314 us (47%)
  Pallas kernels  166 us (25%)
  blocking collectives  63 us (9%)
  matrix products  55.9 us (8%)
  local copies, waits for them, and re-layouts  22.4 us (3%)
  between operations  16.3 us (2%)
  other arithmetic  15.6 us (2%)
    pallas_call x1, Pallas kernels, run_gather(): pl.pallas_call(gather_kernel, in_specs=[pl.BlockSpec(memory_space=pl.ANY)...  126 us
    reduce_scatter x1, waiting for transfers between devices, head_plan(): lax.psum_scatter(d_normed.reshape(n_own, length, width), 'seq', scatter_d...  97.4 us
    reduce_scatter x1, waiting for transfers between devices, head_plan(): grad_in = lax.psum_scatter(grad_in, 'dp', scatter_dimension=0, tiled=True)  65.9 us
    reduce_scatter x1, waiting for transfers between devices, head_plan(): lax.psum_scatter(grad_in[:, 2 * chan:], 'seq', scatter_dimension=0, tiled...  58.4 us
    reduce_scatter x1, waiting for transfers between devices, head_plan(): lax.psum_scatter(part.reshape(n_own, length, width), 'seq', scatter_dimen...  48.4 us
    reduce_scatter x1, waiting for transfers between devices, head_plan(): grad_out = lax.psum_scatter(grad_out, 'dp', scatter_dimension=0, tiled=True)  44.2 us
    psum x1, blocking collectives, head_plan(): lax.psum((jnp.concatenate([spread_chan(g_x[:CONV].T), g_bc[:CONV].T], axi...  44.1 us
    pallas_call x1, Pallas kernels, run_backward(): pl.pallas_call(functools.partial(scan_backward, h_own, n_seq, heads_row),...  27.1 us
  transfers between devices with their start and end apart: 7, of which 5 were waited for; matrix products, arithmetic and copies ran while one was open for 7% of the time, Pallas kernels for 0%

profile of v3, /device:TPU:0, one launch (start us, length us, event | category | flops | bytes accessed | tf_op | source)
XLA Modules:
  0.0 659.6 jit_solution(10929858169012945396)
XLA Ops:
  10.0 2.0 fusion.9.normed
  12.6 125.9 %gather.1 = (bf16[2,512,2048]{2,1,0:T(8,128)(2,1)}, bf16[2,512,2048]{2,1,0:T(8,128)(2,1)}, bf16[2048,1344]{1,0:T(8,128)(2,1)}, bf16[512,2048]{1,0:T(8,128)(2,1)}, f32[8,8,128]{2,1,0:T(8,128)}) custom-call(bf16[2,64,2048]{2,1,0:T(8,128)(2,1)} %fusion.9.normed, bf16[2,64,2048]{2,1,0:T(8,128)(2,1)} %cot.1, bf16[64,8512]{1,0:T(8,128)(2,1)} %in_w.1, ...), custom_call_target="tpu_custom_call" | custom-call | tf_op jit(solution)/shard_map/gather/pallas_call | solution.py:848
  138.5 11.7 %fusion.22 = (bf16[1024,1344]{1,0:T(8,128)(2,1)S(1)}, f32[1024,1344]{1,0:T(8,128)}) fusion(bf16[1024,2048]{1,0:T(8,128)(2,1)} %bitcast.117, bf16[2048,1344]{1,0:T(8,128)(2,1)} %get-tuple-element.25), kind=kOutput, calls=%fused_computation.76 | convolution fusion | flops 5638520832 | bytes 17956864 | tf_op jit(solution)/shard_map/dot_general | solution.py:929
  153.1 12.8 %scan_forward.1 = (bf16[1024,512]{1,0:T(8,128)(2,1)S(1)}, f32[1024,512]{1,0:T(8,128)S(1)}) custom-call(bf16[1024,512]{1,0:T(8,128)(2,1)S(1)} %slice.87.x_ref, bf16[1024,256]{1,0:T(8,128)(2,1)S(1)} %slice.88.bc_ref, bf16[1024,64]{1,0:T(8,128)(2,1)S(1)} %slice.89.dt_ref, f32[2,512,1]{2,1,0:T(8,128)S(1)} %broadcast_in_dim_reshape.18.segc_ref, ...), custom_call_target="tpu_custom_call" | custom-call | tf_op jit(solution)/shard_map/scan_forward/pallas_call | solution.py:548
  166.0 7.7 %multiply_reduce_fusion.2 = (f32[1024]{0:T(1024)S(1)}, f32[1024]{0:T(1024)S(1)}, f32[1024,512]{1,0:T(8,128)}) fusion(bf16[1024,512]{1,0:T(8,128)(2,1)S(1)} %get-tuple-element.27, f32[1024,1344]{1,0:T(8,128)} %get-tuple-element.59, f32[512]{0:T(512)S(1)} %bitcast.107, bf16[1024,2048]{1,0:T(8,128)(2,1)} %bitcast.115, bf16[512,2048]{1,0:T(8,128)(2,1)S(1)} %copy-done.22), kind=kOutput, calls=%fused_computation.19 | convolution fusion | flops 2153248768 | bytes 11544576 | tf_op jit(solution)/shard_map/dot_general | solution.py:954
  173.8 18.9 %psum.56 = f32[2,1024]{1,0:T(2,128)S(1)} all-reduce(f32[2,1024]{1,0:T(2,128)S(1)} %pad_maximum_fusion.6), channel_id=1, replica_groups=mesh['dp'=4,'seq'=8] {'seq'}, use_global_device_ids=true, to_apply=%region_3.4 | all-reduce | flops 2048 | bytes 16384 | tf_op jit(solution)/shard_map/psum | solution.py:958
  192.8 4.2 fusion.1
  197.0 27.1 %scan_backward.1 = (bf16[1024,512]{1,0:T(8,128)(2,1)}, bf16[1024,256]{1,0:T(8,128)(2,1)}, f32[1024,128]{1,0:T(8,128)}, f32[2,8,512]{2,1,0:T(8,128)}, f32[2,8,256]{2,1,0:T(8,128)}, /*index=5*/f32[2,8,128]{2,1,0:T(8,128)}) custom-call(bf16[1024,512]{1,0:T(8,128)(2,1)} %copy-done.2, bf16[1024,256]{1,0:T(8,128)(2,1)} %copy-done.3, bf16[1024,64]{1,0:T(8,128)(2,1)} %copy-done.5, ...), custom_call_target="tpu_custom_call" | custom-call | tf_op jit(solution)/shard_map/scan_backward/pallas_call | solution.py:568
  225.7 10.6 %fusion.14 = f32[2048,1344]{0,1:T(8,128)} fusion(bf16[1024,2048]{1,0:T(8,128)(2,1)} %bitcast.118, bf16[1024,64]{1,0:T(8,128)(2,1)S(1)} %bitcast.88, bf16[1024,256]{1,0:T(8,128)(2,1)} %get-tuple-element.32, bf16[1024,512]{1,0:T(8,128)(2,1)} %get-tuple-element.31, bf16[1024,512]{1,0:T(8,128)(2,1)S(1)} %get-tuple-element.49), kind=kOutput, calls=%fused_computation.35 | convolution fusion | flops 5648154624 | bytes 17956864 | tf_op jit(solution)/shard_map/td,tf->df/dot_general | solution.py:993
  237.4 11.3 %convolution_convert_fusion = bf16[1024,2048]{1,0:T(8,128)(2,1)} fusion(bf16[2048,1344]{1,0:T(8,128)(2,1)} %get-tuple-element.25, bf16[1024,64]{1,0:T(8,128)(2,1)S(1)} %bitcast.89, bf16[1024,256]{1,0:T(8,128)(2,1)S(1)} %copy-done.23, bf16[1024,512]{1,0:T(8,128)(2,1)} %get-tuple-element.31, bf16[1024,512]{1,0:T(8,128)(2,1)S(1)} %get-tuple-element.49), kind=kOutput, calls=%fused_computation | convolution fusion | flops 5650251776 | bytes 12451840 | tf_op jit(solution)/shard_map/dot_general | solution.py:987
  248.7 7.3 %convolution_convert_fusion.1 = bf16[1024,2048]{1,0:T(8,128)(2,1)} fusion(bf16[512,2048]{1,0:T(8,128)(2,1)} %get-tuple-element.29, f32[1024]{0:T(1024)S(1)} %bitcast.97, f32[512]{0:T(512)S(1)} %bitcast.109, bf16[1024,512]{1,0:T(8,128)(2,1)S(1)} %get-tuple-element.27, f32[1024,1344]{1,0:T(8,128)} %get-tuple-element.59), kind=kOutput, calls=%fused_computation.1 | convolution fusion | flops 2154299392 | bytes 9443328 | tf_op jit(solution)/shard_map/dot_general | solution.py:963
  256.1 65.9 %reduce-scatter.12.cloned.1.call-done = f32[512,1344]{0,1:T(8,128)} async-done(((f32[2048,1344]{0,1:T(8,128)}), f32[512,1344]{0,1:T(8,128)}) %reduce-scatter.12.cloned.1.call-update) | async-done | bytes 2752528 | tf_op jit(solution)/shard_map/reduce_scatter | solution.py:994
  325.3 7.3 %fusion.21 = f32[512,2048]{1,0:T(8,128)} fusion(bf16[1024,2048]{1,0:T(8,128)(2,1)} %bitcast.116, f32[1024]{0:T(1024)S(1)} %bitcast.98, f32[512]{0:T(512)S(1)} %bitcast.110, bf16[1024,512]{1,0:T(8,128)(2,1)S(1)} %get-tuple-element.27, f32[1024,1344]{1,0:T(8,128)} %get-tuple-element.59), kind=kOutput, calls=%fused_computation.75 | convolution fusion | flops 2152202240 | bytes 11540480 | tf_op jit(solution)/shard_map/tf,td->fd/dot_general | solution.py:972
  334.3 2.4 reshape.177
  336.6 3.8 copy.85
  340.5 5.8 all-to-all-start
  347.3 97.4 %reduce-scatter.10.cloned.1.call-done = bf16[2,64,2048]{2,1,0:T(8,128)(2,1)} async-done(((bf16[2,512,2048]{2,1,0:T(8,128)(2,1)}), bf16[2,64,2048]{2,1,0:T(8,128)(2,1)}) %reduce-scatter.10.cloned.1.call-update) | async-done | bytes 524304 | tf_op jit(solution)/shard_map/reduce_scatter | solution.py:990
  446.1 44.1 %all-reduce.2 = (f32[4352]{0:T(1024)}, f32[64]{0:T(128)}, f32[64]{0:T(128)}, f32[64]{0:T(128)}, f32[2048]{0:T(1024)}, /*index=5*/f32[4096]{0:T(1024)}) all-reduce(f32[4352]{0:T(1024)S(1)} %pad_maximum_fusion.5, f32[64]{0:T(128)S(1)} %reshape.171, f32[64]{0:T(128)S(1)} %reshape.172, ...), channel_id=1, replica_groups=mesh['dp'=4,'seq'=8] {'dp','seq'}, use_global_device_ids=true, to_apply=%region_12.13 | all-reduce | flops 10688 | bytes 85504 | tf_op jit(solution)/shard_map/psum | solution.py:1006
  490.2 48.4 %reduce-scatter.8.cloned.1.call-done = bf16[2,64,2048]{2,1,0:T(8,128)(2,1)} async-done(((bf16[2,512,2048]{2,1,0:T(8,128)(2,1)}), bf16[2,64,2048]{2,1,0:T(8,128)(2,1)}) %reduce-scatter.8.cloned.1.call-update) | async-done | bytes 524304 | tf_op jit(solution)/shard_map/reduce_scatter | solution.py:964
  538.6 2.7 fusion.6
  541.3 2.5 copy.86
  545.6 58.4 %reduce-scatter.16.cloned.1.call-done = f32[64,320]{1,0:T(8,128)} async-done(((f32[512,320]{1,0:T(8,128)}), f32[64,320]{1,0:T(8,128)}) %reduce-scatter.16.cloned.1.call-update) | async-done | bytes 81936 | tf_op jit(solution)/shard_map/reduce_scatter | solution.py:998
  603.9 2.4 pad_maximum_fusion.1
  606.3 44.2 %reduce-scatter.14.cloned.1.call-done = f32[128,2048]{1,0:T(8,128)} async-done(((f32[512,2048]{1,0:T(8,128)}), f32[128,2048]{1,0:T(8,128)}) %reduce-scatter.14.cloned.1.call-update) | async-done | bytes 1048592 | tf_op jit(solution)/shard_map/reduce_scatter | solution.py:973
  (150 shorter events, 18.5 us)
Async XLA Ops:
  8.0 144.9 %copy-start = (f32[4096]{0:T(1024)S(1)}, f32[4096]{0:T(1024)}, u32[]{:S(2)}) copy-start(f32[4096]{0:T(1024)} %param.21) | copy-start | bytes 49156
  8.0 314.0 %reduce-scatter.12.cloned.1.call-start = ((), (), s32[]{:S(2)}) async-start(), calls=%async_computation.8 | async-start | bytes 13762560 | tf_op jit(solution)/shard_map/reduce_scatter | solution.py:994
  150.4 15.6 %copy-start.2 = (bf16[1024,512]{1,0:T(8,128)(2,1)}, bf16[1024,512]{1,0:T(8,128)(2,1)S(1)}, u32[]{:S(2)}) copy-start(bf16[1024,512]{1,0:T(8,128)(2,1)S(1)} %slice.87.x_ref) | copy-start | bytes 3145732
  150.4 23.3 %copy-start.3 = (bf16[1024,256]{1,0:T(8,128)(2,1)}, bf16[1024,256]{1,0:T(8,128)(2,1)S(1)}, u32[]{:S(2)}) copy-start(bf16[1024,256]{1,0:T(8,128)(2,1)S(1)} %slice.88.bc_ref) | copy-start | bytes 1572868
  150.5 23.3 %copy-start.5 = (bf16[1024,64]{1,0:T(8,128)(2,1)}, bf16[1024,64]{1,0:T(8,128)(2,1)S(1)}, u32[]{:S(2)}) copy-start(bf16[1024,64]{1,0:T(8,128)(2,1)S(1)} %slice.89.dt_ref) | copy-start | bytes 393220
  151.8 21.9 %copy-start.4 = (f32[2,512,1]{2,1,0:T(8,128)}, f32[2,512,1]{2,1,0:T(8,128)S(1)}, u32[]{:S(2)}) copy-start(f32[2,512,1]{2,1,0:T(8,128)S(1)} %broadcast_in_dim_reshape.18.segc_ref) | copy-start | bytes 12292
  151.9 21.8 %copy-start.9 = (f32[2,1,512]{2,1,0:T(1,128)}, f32[2,1,512]{2,1,0:T(1,128)S(1)}, u32[]{:S(2)}) copy-start(f32[2,1,512]{2,1,0:T(1,128)S(1)} %broadcast_in_dim_reshape.15.segr_ref) | copy-start | bytes 12292
  152.9 13.0 %copy-start.22 = (bf16[512,2048]{1,0:T(8,128)(2,1)S(1)}, bf16[512,2048]{1,0:T(8,128)(2,1)}, u32[]{:S(2)}) copy-start(bf16[512,2048]{1,0:T(8,128)(2,1)} %get-tuple-element.29) | copy-start | bytes 6291460
  153.0 20.8 %copy-start.10 = (f32[8,128]{1,0:T(8,128)}, f32[8,128]{1,0:T(8,128)S(1)}, u32[]{:S(2)}) copy-start(f32[8,128]{1,0:T(8,128)S(1)} %select_maximum_fusion.head_ref) | copy-start | bytes 12292
  153.1 20.7 %copy-start.8 = (f32[8,256]{1,0:T(8,128)}, f32[8,256]{1,0:T(8,128)S(1)}, u32[]{:S(2)}) copy-start(f32[8,256]{1,0:T(8,128)S(1)} %maximum_maximum_fusion.1.wbc_ref) | copy-start | bytes 24580
  153.1 20.6 %copy-start.7 = (f32[8,512]{1,0:T(8,128)}, f32[8,512]{1,0:T(8,128)S(1)}, u32[]{:S(2)}) copy-start(f32[8,512]{1,0:T(8,128)S(1)} %maximum_maximum_fusion.wx_ref) | copy-start | bytes 49156
  166.0 7.8 %copy-start.6 = (f32[1024,512]{1,0:T(8,128)}, f32[1024,512]{1,0:T(8,128)S(1)}, u32[]{:S(2)}) copy-start(f32[1024,512]{1,0:T(8,128)S(1)} %get-tuple-element.30.inner_ref) | copy-start | bytes 6291460
  236.4 208.4 %reduce-scatter.10.cloned.1.call-start = ((), (), s32[]{:S(2)}) async-start(), calls=%async_computation.7 | async-start | bytes 4718592 | tf_op jit(solution)/shard_map/reduce_scatter | solution.py:990
  248.7 289.9 %reduce-scatter.8.cloned.1.call-start = ((), (), s32[]{:S(2)}) async-start(), calls=%async_computation.6 | async-start | bytes 4718592 | tf_op jit(solution)/shard_map/reduce_scatter | solution.py:964
  256.1 68.3 %copy-start.15 = (f32[2,8,512]{2,1,0:T(8,128)S(1)}, f32[2,8,512]{2,1,0:T(8,128)}, u32[]{:S(2)}) copy-start(f32[2,8,512]{2,1,0:T(8,128)} %get-tuple-element.34) | copy-start | bytes 98308
  256.1 68.5 %copy-start.16 = (f32[2,8,256]{2,1,0:T(8,128)S(1)}, f32[2,8,256]{2,1,0:T(8,128)}, u32[]{:S(2)}) copy-start(f32[2,8,256]{2,1,0:T(8,128)} %get-tuple-element.35) | copy-start | bytes 49156
  256.1 347.9 %reduce-scatter.16.cloned.1.call-start = ((), (), s32[]{:S(2)}) async-start(), calls=%async_computation.11 | async-start | bytes 884736 | tf_op jit(solution)/shard_map/reduce_scatter | solution.py:998
  324.3 282.0 %all-reduce.5.cloned.1.call-start = ((), (), s32[]{:S(2)}) async-start(), calls=%async_computation.9 | async-start | bytes 139264 | tf_op jit(solution)/shard_map/psum | solution.py:1006
  325.2 325.3 %reduce-scatter.14.cloned.1.call-start = ((), (), s32[]{:S(2)}) async-start(), calls=%async_computation.10 | async-start | bytes 5242880 | tf_op jit(solution)/shard_map/reduce_scatter | solution.py:973
  340.5 104.3 %copy-start.11 = (bf16[2,64,2048]{2,1,0:T(8,128)(2,1)S(1)}, bf16[2,64,2048]{2,1,0:T(8,128)(2,1)}, u32[]{:S(2)}) copy-start(bf16[2,64,2048]{2,1,0:T(8,128)(2,1)} %param.12) | copy-start | bytes 1572868
  340.5 104.3 %copy-start.13 = (f32[2048]{0:T(1024)S(1)}, f32[2048]{0:T(1024)}, u32[]{:S(2)}) copy-start(f32[2048]{0:T(1024)} %param.20) | copy-start | bytes 24580
  340.5 198.1 %copy-start.12 = (bf16[2,64,2048]{2,1,0:T(8,128)(2,1)S(1)}, bf16[2,64,2048]{2,1,0:T(8,128)(2,1)}, u32[]{:S(2)}) copy-start(bf16[2,64,2048]{2,1,0:T(8,128)(2,1)} %cot.1) | copy-start | bytes 1572868
  340.5 200.8 %all-to-all-start = ((f32[8,64,2,4,1,128]{5,3,2,1,4,0:T(4,128)}), f32[8,64,2,4,1,128]{5,3,2,1,4,0:T(4,128)S(1)}, u32[]{:S(2)}, u32[]{:S(2)}) async-start(f32[8,64,2,4,1,128]{5,3,2,1,4,0:T(4,128)} %copy.85), calls=%async_computation.3 | async-start | bytes 4194304 | tf_op jit(solution)/shard_map/all_to_all | solution.py:996
  543.8 108.3 %copy-start.1 = (f32[4096]{0:T(1024)S(1)}, f32[4096]{0:T(1024)}, u32[]{:S(2)}) copy-start(f32[4096]{0:T(1024)} %param.21) | copy-start | bytes 49156
  (9 other events, 20.9 us)
Sparse Core Ops, SparseCore 0:
  236.5 85.4 reduce-scatter.11
  325.6 119.0 reduce-scatter.9
  448.8 89.7 reduce-scatter.7
  541.8 62.1 reduce-scatter.15
  607.1 43.4 reduce-scatter.13
Sparse Core Ops, SparseCore 1:
  331.9 194.9 all-reduce.4
